TPU v7x, 256 devices: a whole 4x4x8 slice. The times are simulated.
256 devices in a mesh: blk: 64 (over x, y, z_hi, core), grp: 4 (over z_lo).
Axes of the slice: x: 4, y: 4, z: 8 (z_hi: 2, z_lo: 4; z = z_hi * 4 + z_lo), core: 2. Of those that a mesh axis runs over, the one named last changes fastest.
Arguments:
- generated: bfloat16 [40960, 2048], P('blk', 'grp'), may hold values from -6 to 6
- reference_set: bfloat16 [40960, 2048], P('blk', 'grp'), may hold values from -6 to 6
- partners: int32 [2, 64], replicated, may hold values from 0 to 63, as said below
Outputs:
- proof: float32 [40960], P('blk')
- feature_grads: float32 [40960, 2048], P('blk', 'grp')
Inputs may be any that keep to these rules, and one draw needn't show every extreme that they name: In each round every block's partner is its own index with one fixed nonzero set of bits flipped, the same set for all blocks of that round; the sets of the 2 rounds differ, so partners pair up and no block meets the same partner twice.
All inputs are finite; a program needn't handle non-finite values.
Results may differ from a plain program's by a relative error of at most 0.0026.
Values may be sent and summed in bfloat16 or wider, within the bound.
No kernel may reach another device: no remote copies, remote signals or barrier semaphores. Data moves between devices by JAX's collectives and lax.ppermute only.
A program may use at most 64 MiB of HBM per device.

v0:
```python
import jax
import jax.numpy as jnp
from jax import lax
from jax.experimental import pallas as pl
from jax.experimental.pallas import tpu as pltpu
from jax.sharding import PartitionSpec as P

TILE = 128
CORE, FAR = 1, 2


def grp_swap(value, distance):
    size = lax.axis_size("grp")
    return lax.ppermute(value, "grp", [(k, k ^ distance) for k in range(size)])


def blk_swap(value, mask):
    blocks = lax.axis_size("blk")
    return lax.ppermute(value, "blk", [(b, b ^ mask) for b in range(blocks)])


def far_swap(value):
    blocks, groups = lax.axis_size("blk"), lax.axis_size("grp")
    pairs = [
        (b * groups + k, (b ^ FAR) * groups + groups - 1 - k)
        for b in range(blocks)
        for k in range(groups)
    ]
    return lax.ppermute(value, ("blk", "grp"), pairs)


def plane_hop(value, step):
    stride = 2 * FAR
    masks = range(stride, lax.axis_size("blk"), stride)
    branches = [lambda v, m=m: blk_swap(v, m) for m in masks]
    return lax.switch(step, [lambda v: v] + branches, value)


def tile_kernel(full_width, grad_scale, wit_scale, first, *refs):
    slots = len(refs) // 2 - 1
    left = refs[:slots]
    met, proof, *grads = refs[slots:]
    total = [jnp.zeros(g.shape, jnp.float32) for g in grads]
    witness = jnp.zeros(proof.shape, jnp.float32)
    for index in range(met.shape[0]):
        count = met.shape[2]
        gram = jnp.zeros((TILE, count), jnp.float32)
        for slot in range(slots):
            gram += lax.dot_general(
                left[slot][...],
                met[index, slot ^ first[0]],
                (((1,), (1,)), ((), ())),
                preferred_element_type=jnp.float32,
            )
        column = lax.broadcasted_iota(jnp.int32, gram.shape, 1)
        sign = jnp.where(column < count // 2, 1.0, -1.0)
        shifted = gram * (1.0 / full_width) + 1.0
        squared = shifted * shifted
        signed = squared * sign
        witness += jnp.sum(signed * shifted, axis=1, keepdims=True)
        weight = (3.0 * signed).astype(jnp.bfloat16)
        for slot in range(slots):
            total[slot] += jnp.dot(
                weight, met[index, slot ^ first[0]], preferred_element_type=jnp.float32
            )
    proof[...] = witness * wit_scale
    for slot in range(slots):
        grads[slot][...] = (total[slot] * grad_scale).astype(grads[slot].dtype)


def on_device(generated, reference_set, partners):
    block_rows, feat_width = generated.shape
    groups = lax.axis_size("grp")
    full_width = feat_width * groups
    rounds_count = partners.shape[0]
    share = block_rows // groups
    wit_scale = (full_width / (rounds_count * block_rows)) ** 0.5
    grad_scale = 1.0 / (rounds_count * block_rows) ** 0.5
    here = lax.axis_index("grp")

    both = jnp.concatenate(
        [
            generated.reshape(groups, share, feat_width),
            reference_set.reshape(groups, share, feat_width),
        ],
        axis=1,
    )
    own_rows = lax.all_to_all(both, "grp", 0, 0)
    own_rows, generated = lax.optimization_barrier((own_rows, generated))
    left = [generated] + [grp_swap(generated, d) for d in range(1, groups)]

    masks = partners[:, 0]
    any_far = jnp.any(masks & FAR > 0)
    far_rows = lax.cond(any_far, far_swap, lambda v: v, own_rows)

    def meet(carry, mask):
        rows = jnp.where(mask & FAR > 0, far_rows, own_rows)
        rows = lax.cond(mask & CORE > 0, lambda v: blk_swap(v, CORE), lambda v: v, rows)
        return carry, plane_hop(rows, mask // (2 * FAR))

    _, met = lax.scan(meet, 0, masks)
    first = here.astype(jnp.int32).reshape(1)

    tile = pl.BlockSpec((TILE, feat_width), lambda i: (i, 0))
    whole = pl.BlockSpec(met.shape, lambda i: (0, 0, 0, 0))
    out = pl.pallas_call(
        lambda *refs: tile_kernel(full_width, grad_scale, wit_scale, *refs),
        grid=(block_rows // TILE,),
        in_specs=[pl.BlockSpec(memory_space=pltpu.SMEM)]
        + [tile] * groups
        + [whole],
        out_specs=[pl.BlockSpec((TILE, 1), lambda i: (i, 0))] + [tile] * groups,
        out_shape=[jax.ShapeDtypeStruct((block_rows, 1), jnp.float32)]
        + [
            jax.ShapeDtypeStruct(
                (block_rows, feat_width), jnp.bfloat16 if d else jnp.float32
            )
            for d in range(groups)
        ],
        compiler_params=pltpu.CompilerParams(vmem_limit_bytes=40 * 2**20),
    )(first, *left, met)
    proof = out[0].reshape(block_rows)
    for distance in (1, 2):
        proof = proof + grp_swap(proof, distance)
    grads = out[1]
    for distance in range(1, groups):
        grads = grads + grp_swap(out[1 + distance], distance).astype(jnp.float32)
    return (proof, grads)


def solution(mesh):
    return jax.shard_map(
        on_device,
        mesh=mesh,
        in_specs=(P("blk", "grp"), P("blk", "grp"), P()),
        out_specs=(P("blk"), P("blk", "grp")),
        check_vma=False,
    )
```

profile of v0, /device:TPU:6, one launch (start us, length us, event | category | flops | bytes accessed | tf_op | source)
XLA Modules:
  0.0 284.0 jit_solution(7222014851448543016)
XLA Ops:
  0.6 2.4 pad_maximum_fusion
  3.1 6.0 %all-to-all-start = ((bf16[4,320,512]{2,1,0:T(8,128)(2,1)}), bf16[4,320,512]{2,1,0:T(8,128)(2,1)}, u32[]{:S(2)}, u32[]{:S(2)}) async-start(bf16[4,320,512]{2,1,0:T(8,128)(2,1)} %pad_maximum_fusion), calls=%async_computation | async-start | bytes 2621440 | tf_op jit(solution)/shard_map/all_to_all | solution.py:88
  10.5 30.0 %all-to-all-done = bf16[4,320,512]{2,1,0:T(8,128)(2,1)} async-done(((bf16[4,320,512]{2,1,0:T(8,128)(2,1)}), bf16[4,320,512]{2,1,0:T(8,128)(2,1)}, u32[]{:S(2)}, u32[]{:S(2)}) %all-to-all-start) | async-done | bytes 1310752 | tf_op jit(solution)/shard_map/all_to_all | solution.py:88
  44.9 35.1 %conditional.3 = (bf16[4,320,512]{2,1,0:T(8,128)(2,1)}) conditional(s32[]{:T(128)} %convert_element_type.18, bf16[4,320,512]{2,1,0:T(8,128)(2,1)} %all-to-all-done, bf16[4,320,512]{2,1,0:T(8,128)(2,1)} %all-to-all-done), branch_computations={%region_1.0_spmd, %region_2.0_spmd} | conditional | bytes 5242928 | solution.py:94
  44.9 4.1 %collective-permute-start = (bf16[4,320,512]{2,1,0:T(8,128)(2,1)}, bf16[4,320,512]{2,1,0:T(8,128)(2,1)}, u32[]{:S(2)}, u32[]{:S(2)}) collective-permute-start(bf16[4,320,512]{2,1,0:T(8,128)(2,1)} %param.1), channel_id=1, source_target_pairs={{0,11},{1,10},{2,9},{3,8},{4,15},{5,14},{6,13},{7,12},{8,3},{9,2},... | collective-permute-start | bytes 3932168 | tf_op jit(solution)/shard_map/cond/branch_1_fun/ppermute | solution.py:29
  49.0 31.1 %collective-permute-done = bf16[4,320,512]{2,1,0:T(8,128)(2,1)} collective-permute-done((bf16[4,320,512]{2,1,0:T(8,128)(2,1)}, bf16[4,320,512]{2,1,0:T(8,128)(2,1)}, u32[]{:S(2)}, u32[]{:S(2)}) %collective-permute-start) | collective-permute-done | bytes 1310752 | tf_op jit(solution)/shard_map/cond/branch_1_fun/ppermute | solution.py:29
  80.1 86.9 %while.12 = (s32[]{:T(128)}, bf16[2,4,320,512]{3,2,1,0:T(8,128)(2,1)}, s32[2]{0:T(128)S(1)}, bf16[4,320,512]{2,1,0:T(8,128)(2,1)}, bf16[4,320,512]{2,1,0:T(8,128...) while((s32[]{:T(128)}, ...), condition=%wide.region_22.23_spmd, body=%wide.region_3.22_spmd.sunk | while | flops 655383 | bytes 22283184 | solution.py:101
  83.7 2.5 broadcast_select_fusion.2
  86.9 31.0 %conditional.7 = (bf16[4,320,512]{2,1,0:T(8,128)(2,1)}) conditional(s32[]{:T(128)} %clamp.7, bf16[4,320,512]{2,1,0:T(8,128)(2,1)} %get-tuple-element.230, bf16[4,320,512]{2,1,0:T(8,128)(2,1)} %get-tuple-element.230, bf16[4,320,512]{2,1,0:T(8,128)(2,1)} %get-tuple-element.230, ...), branch_computations={%region_6.6_spmd, %region_7.7_spmd, %region_8.8_spmd, %region_9.9_... | conditional | bytes 7864368 | solution.py:36
  86.9 4.1 %collective-permute-start.11 = (bf16[4,320,512]{2,1,0:T(8,128)(2,1)}, bf16[4,320,512]{2,1,0:T(8,128)(2,1)S(1)}, u32[]{:S(2)}, u32[]{:S(2)}) collective-permute-start(bf16[4,320,512]{2,1,0:T(8,128)(2,1)} %param.14), channel_id=1, source_target_pairs={{0,160},{4,164},{8,168},{12,172},{16,176},{20,180},{24,184},{28,18... | collective-permute-start | bytes 3932168 | tf_op jit(solution)/shard_map/while/body/eval_jaxpr/cond/branch_10_fun/ppermute | solution.py:19
  91.0 25.8 %collective-permute-done.11 = bf16[4,320,512]{2,1,0:T(8,128)(2,1)S(1)} collective-permute-done((bf16[4,320,512]{2,1,0:T(8,128)(2,1)}, bf16[4,320,512]{2,1,0:T(8,128)(2,1)S(1)}, u32[]{:S(2)}, u32[]{:S(2)}) %collective-permute-start.11) | collective-permute-done | bytes 1310752 | tf_op jit(solution)/shard_map/while/body/eval_jaxpr/cond/branch_10_fun/ppermute | solution.py:19
  117.9 2.5 bitcast_dynamic-update-slice_fusion.2
  124.0 2.5 broadcast_select_fusion.2
  127.1 4.4 %conditional.6 = (bf16[4,320,512]{2,1,0:T(8,128)(2,1)}) conditional(s32[]{:T(128)} %convert_element_type.26, bf16[4,320,512]{2,1,0:T(8,128)(2,1)} %broadcast_select_fusion.2, bf16[4,320,512]{2,1,0:T(8,128)(2,1)} %broadcast_select_fusion.2), branch_computations={%region_4.4_spmd, %region_5.5_spmd} | conditional | bytes 7864368 | solution.py:98
  127.2 3.2 %collective-permute-done.1 = bf16[4,320,512]{2,1,0:T(8,128)(2,1)S(1)} collective-permute-done((bf16[4,320,512]{2,1,0:T(8,128)(2,1)}, bf16[4,320,512]{2,1,0:T(8,128)(2,1)S(1)}, u32[]{:S(2)}, u32[]{:S(2)}) %collective-permute-start.1) | collective-permute-done | bytes 1310752 | tf_op jit(solution)/shard_map/while/body/eval_jaxpr/cond/branch_1_fun/ppermute | solution.py:19
  131.5 33.0 %conditional.7 = (bf16[4,320,512]{2,1,0:T(8,128)(2,1)}) conditional(s32[]{:T(128)} %clamp.7, bf16[4,320,512]{2,1,0:T(8,128)(2,1)} %get-tuple-element.230, bf16[4,320,512]{2,1,0:T(8,128)(2,1)} %get-tuple-element.230, bf16[4,320,512]{2,1,0:T(8,128)(2,1)} %get-tuple-element.230, ...), branch_computations={%region_6.6_spmd, %region_7.7_spmd, %region_8.8_spmd, %region_9.9_... | conditional | bytes 7864368 | solution.py:36
  133.4 30.1 %collective-permute-done.6 = bf16[4,320,512]{2,1,0:T(8,128)(2,1)S(1)} collective-permute-done((bf16[4,320,512]{2,1,0:T(8,128)(2,1)}, bf16[4,320,512]{2,1,0:T(8,128)(2,1)S(1)}, u32[]{:S(2)}, u32[]{:S(2)}) %collective-permute-start.6) | collective-permute-done | bytes 1310752 | tf_op jit(solution)/shard_map/while/body/eval_jaxpr/cond/branch_5_fun/ppermute | solution.py:19
  164.5 2.5 bitcast_dynamic-update-slice_fusion.2
  168.9 13.2 %shard_map.50 = (f32[640,1]{1,0:T(8,128)S(1)}, f32[640,512]{1,0:T(8,128)S(1)}, bf16[640,512]{1,0:T(8,128)(2,1)}, bf16[640,512]{1,0:T(8,128)(2,1)}, bf16[640,512]{1,0:T(8,128)(2,1)}) custom-call(s32[1]{0:T(128)} %bitcast.2.refs_0_, bf16[640,512]{1,0:T(8,128)(2,1)S(1)} %copy-done, bf16[640,512]{1,0:T(8,128)(2,1)S(1)} %collective-permute-done.17.refs_2_, ...), custom_call_target="tpu_custom_call" | custom-call | tf_op jit(solution)/shard_map/pallas_call | solution.py:106
  182.8 39.6 %collective-permute-start.22 = (bf16[640,512]{1,0:T(8,128)(2,1)}, bf16[640,512]{1,0:T(8,128)(2,1)S(1)}, u32[]{:S(2)}, u32[]{:S(2)}) collective-permute-start(bf16[640,512]{1,0:T(8,128)(2,1)} %get-tuple-element.132), channel_id=1, source_target_pairs={{0,1},{1,0},{2,3},{3,2},{4,5},{5,4},{6,7},{7,6},{8,9},{9,8},{10,11... | collective-permute-start | bytes 1966088 | tf_op jit(solution)/shard_map/ppermute | solution.py:14
  222.5 2.7 collective-permute-start.23
  228.5 36.0 %collective-permute-done.20 = f32[640]{0:T(1024)S(1)} collective-permute-done((f32[640]{0:T(1024)S(1)}, f32[640]{0:T(1024)S(1)}, u32[]{:S(2)}, u32[]{:S(2)}) %collective-permute-start.20) | collective-permute-done | bytes 2592 | tf_op jit(solution)/shard_map/ppermute | solution.py:14
  264.4 5.2 %collective-permute-start.21 = (f32[640]{0:T(1024)S(1)}, f32[640]{0:T(1024)S(1)}, u32[]{:S(2)}, u32[]{:S(2)}) collective-permute-start(f32[640]{0:T(1024)S(1)} %add.25), channel_id=1, source_target_pairs={{0,2},{1,3},{2,0},{3,1},{4,6},{5,7},{6,4},{7,5},{8,10},{9,11},{10,... | collective-permute-start | bytes 7688 | tf_op jit(solution)/shard_map/ppermute | solution.py:14
  269.6 12.3 %collective-permute-done.21 = f32[640]{0:T(1024)S(1)} collective-permute-done((f32[640]{0:T(1024)S(1)}, f32[640]{0:T(1024)S(1)}, u32[]{:S(2)}, u32[]{:S(2)}) %collective-permute-start.21) | collective-permute-done | bytes 2592 | tf_op jit(solution)/shard_map/ppermute | solution.py:14
  (36 shorter events, 19.4 us)
Async XLA Ops:
  3.1 6.0 %copy-start.4 = (s32[2,64]{1,0:T(2,128)S(1)}, s32[2,64]{1,0:T(2,128)}, u32[]{:S(2)}) copy-start(s32[2,64]{1,0:T(2,128)} %param.27) | copy-start | bytes 1540
  3.1 37.5 %copy-start = (bf16[640,512]{1,0:T(8,128)(2,1)S(1)}, bf16[640,512]{1,0:T(8,128)(2,1)}, u32[]{:S(2)}) copy-start(bf16[640,512]{1,0:T(8,128)(2,1)} %refs_1_) | copy-start | bytes 1966084
  3.1 37.5 %all-to-all-start = ((bf16[4,320,512]{2,1,0:T(8,128)(2,1)}), bf16[4,320,512]{2,1,0:T(8,128)(2,1)}, u32[]{:S(2)}, u32[]{:S(2)}) async-start(bf16[4,320,512]{2,1,0:T(8,128)(2,1)} %pad_maximum_fusion), calls=%async_computation | async-start | bytes 2621440 | tf_op jit(solution)/shard_map/all_to_all | solution.py:88
  40.5 126.4 %collective-permute-start.17 = (bf16[640,512]{1,0:T(8,128)(2,1)S(1)}, bf16[640,512]{1,0:T(8,128)(2,1)S(1)}, u32[]{:S(2)}, u32[]{:S(2)}) collective-permute-start(bf16[640,512]{1,0:T(8,128)(2,1)S(1)} %copy-done), channel_id=1, source_target_pairs={{0,1},{1,0},{2,3},{3,2},{4,5},{5,4},{6,7},{7,6},{8,9},{9,8},{10,11... | collective-permute-start | bytes 1966088 | tf_op jit(solution)/shard_map/ppermute | solution.py:14
  40.5 126.4 %collective-permute-start.18 = (bf16[640,512]{1,0:T(8,128)(2,1)S(1)}, bf16[640,512]{1,0:T(8,128)(2,1)S(1)}, u32[]{:S(2)}, u32[]{:S(2)}) collective-permute-start(bf16[640,512]{1,0:T(8,128)(2,1)S(1)} %copy-done), channel_id=1, source_target_pairs={{0,2},{1,3},{2,0},{3,1},{4,6},{5,7},{6,4},{7,5},{8,10},{9,11},{10,... | collective-permute-start | bytes 1966088 | tf_op jit(solution)/shard_map/ppermute | solution.py:14
  42.6 124.4 %collective-permute-start.19 = (bf16[640,512]{1,0:T(8,128)(2,1)S(1)}, bf16[640,512]{1,0:T(8,128)(2,1)S(1)}, u32[]{:S(2)}, u32[]{:S(2)}) collective-permute-start(bf16[640,512]{1,0:T(8,128)(2,1)S(1)} %copy-done), channel_id=1, source_target_pairs={{0,3},{1,2},{2,1},{3,0},{4,7},{5,6},{6,5},{7,4},{8,11},{9,10},{10,... | collective-permute-start | bytes 1966088 | tf_op jit(solution)/shard_map/ppermute | solution.py:14
  44.9 35.1 %collective-permute-start = (bf16[4,320,512]{2,1,0:T(8,128)(2,1)}, bf16[4,320,512]{2,1,0:T(8,128)(2,1)}, u32[]{:S(2)}, u32[]{:S(2)}) collective-permute-start(bf16[4,320,512]{2,1,0:T(8,128)(2,1)} %param.1), channel_id=1, source_target_pairs={{0,11},{1,10},{2,9},{3,8},{4,15},{5,14},{6,13},{7,12},{8,3},{9,2},... | collective-permute-start | bytes 3932168 | tf_op jit(solution)/shard_map/cond/branch_1_fun/ppermute | solution.py:29
  86.9 29.9 %collective-permute-start.11 = (bf16[4,320,512]{2,1,0:T(8,128)(2,1)}, bf16[4,320,512]{2,1,0:T(8,128)(2,1)S(1)}, u32[]{:S(2)}, u32[]{:S(2)}) collective-permute-start(bf16[4,320,512]{2,1,0:T(8,128)(2,1)} %param.14), channel_id=1, source_target_pairs={{0,160},{4,164},{8,168},{12,172},{16,176},{20,180},{24,184},{28,18... | collective-permute-start | bytes 3932168 | tf_op jit(solution)/shard_map/while/body/eval_jaxpr/cond/branch_10_fun/ppermute | solution.py:19
  127.1 3.3 %collective-permute-start.1 = (bf16[4,320,512]{2,1,0:T(8,128)(2,1)}, bf16[4,320,512]{2,1,0:T(8,128)(2,1)S(1)}, u32[]{:S(2)}, u32[]{:S(2)}) collective-permute-start(bf16[4,320,512]{2,1,0:T(8,128)(2,1)} %param.3), channel_id=1, source_target_pairs={{0,4},{4,0},{8,12},{12,8},{16,20},{20,16},{24,28},{28,24},{32,36},... | collective-permute-start | bytes 3932168 | tf_op jit(solution)/shard_map/while/body/eval_jaxpr/cond/branch_1_fun/ppermute | solution.py:19
  131.5 31.9 %collective-permute-start.6 = (bf16[4,320,512]{2,1,0:T(8,128)(2,1)}, bf16[4,320,512]{2,1,0:T(8,128)(2,1)S(1)}, u32[]{:S(2)}, u32[]{:S(2)}) collective-permute-start(bf16[4,320,512]{2,1,0:T(8,128)(2,1)} %param.9), channel_id=1, source_target_pairs={{0,80},{4,84},{8,88},{12,92},{16,64},{20,68},{24,72},{28,76},{32,1... | collective-permute-start | bytes 3932168 | tf_op jit(solution)/shard_map/while/body/eval_jaxpr/cond/branch_5_fun/ppermute | solution.py:19
  167.0 0.8 copy-start.1
  167.8 1.1 copy-start.2
  182.1 0.7 copy-start.3
  182.8 99.7 %collective-permute-start.22 = (bf16[640,512]{1,0:T(8,128)(2,1)}, bf16[640,512]{1,0:T(8,128)(2,1)S(1)}, u32[]{:S(2)}, u32[]{:S(2)}) collective-permute-start(bf16[640,512]{1,0:T(8,128)(2,1)} %get-tuple-element.132), channel_id=1, source_target_pairs={{0,1},{1,0},{2,3},{3,2},{4,5},{5,4},{6,7},{7,6},{8,9},{9,8},{10,11... | collective-permute-start | bytes 1966088 | tf_op jit(solution)/shard_map/ppermute | solution.py:14
  222.5 60.1 %collective-permute-start.23 = (bf16[640,512]{1,0:T(8,128)(2,1)}, bf16[640,512]{1,0:T(8,128)(2,1)S(1)}, u32[]{:S(2)}, u32[]{:S(2)}) collective-permute-start(bf16[640,512]{1,0:T(8,128)(2,1)} %get-tuple-element.133), channel_id=1, source_target_pairs={{0,2},{1,3},{2,0},{3,1},{4,6},{5,7},{6,4},{7,5},{8,10},{9,11},{10,... | collective-permute-start | bytes 1966088 | tf_op jit(solution)/shard_map/ppermute | solution.py:14
  225.2 57.4 %collective-permute-start.24 = (bf16[640,512]{1,0:T(8,128)(2,1)}, bf16[640,512]{1,0:T(8,128)(2,1)S(1)}, u32[]{:S(2)}, u32[]{:S(2)}) collective-permute-start(bf16[640,512]{1,0:T(8,128)(2,1)} %get-tuple-element.134), channel_id=1, source_target_pairs={{0,3},{1,2},{2,1},{3,0},{4,7},{5,6},{6,5},{7,4},{8,11},{9,10},{10,... | collective-permute-start | bytes 1966088 | tf_op jit(solution)/shard_map/ppermute | solution.py:14
  227.8 36.6 %collective-permute-start.20 = (f32[640]{0:T(1024)S(1)}, f32[640]{0:T(1024)S(1)}, u32[]{:S(2)}, u32[]{:S(2)}) collective-permute-start(f32[640]{0:T(1024)S(1)} %reduce.1), channel_id=1, source_target_pairs={{0,1},{1,0},{2,3},{3,2},{4,5},{5,4},{6,7},{7,6},{8,9},{9,8},{10,11... | collective-permute-start | bytes 7688 | tf_op jit(solution)/shard_map/ppermute | solution.py:14
  264.4 17.5 %collective-permute-start.21 = (f32[640]{0:T(1024)S(1)}, f32[640]{0:T(1024)S(1)}, u32[]{:S(2)}, u32[]{:S(2)}) collective-permute-start(f32[640]{0:T(1024)S(1)} %add.25), channel_id=1, source_target_pairs={{0,2},{1,3},{2,0},{3,1},{4,6},{5,7},{6,4},{7,5},{8,10},{9,11},{10,... | collective-permute-start | bytes 7688 | tf_op jit(solution)/shard_map/ppermute | solution.py:14
where the time goes:
time: 288 us; the launch traced here: 284 us
  waiting for transfers between devices  169 us (59%)
  starting transfers between devices  70.2 us (24%)
  Pallas kernels  13.2 us (5%)
  local copies, waits for them, and re-layouts  12.1 us (4%)
  other arithmetic  11.2 us (4%)
  loops' own time  7.41 us (3%)
    ppermute x3, waiting for transfers between devices, blk_swap(): return lax.ppermute(value, 'blk', [(b, b ^ mask) for b in range(blocks)])  59.1 us
    ppermute x8, starting transfers between devices, grp_swap(): return lax.ppermute(value, 'grp', [(k, k ^ distance) for k in range(size)])  54 us
    ppermute x8, waiting for transfers between devices, grp_swap(): return lax.ppermute(value, 'grp', [(k, k ^ distance) for k in range(size)])  48.4 us
    ppermute x1, waiting for transfers between devices, far_swap(): return lax.ppermute(value, ('blk', 'grp'), pairs)  31.1 us
    all_to_all x1, waiting for transfers between devices, on_device(): own_rows = lax.all_to_all(both, 'grp', 0, 0)  30 us
    pallas_call x1, Pallas kernels, on_device(): pl.pallas_call(lambda *refs: tile_kernel(full_width, grad_scale, wit_scal...  13.2 us
    another operation x1, loops' own time, on_device(): _, met = lax.scan(meet, 0, masks)  7.33 us
    ppermute x3, starting transfers between devices, blk_swap(): return lax.ppermute(value, 'blk', [(b, b ^ mask) for b in range(blocks)])  6.06 us
  transfers between devices with their start and end apart: 13, of which 7 were waited for; matrix products, arithmetic and copies ran while one was open for 6% of the time, Pallas kernels for 0%

commit v1 on v0

v1 whole, which is shorter than its diff:
```python
import jax
import jax.numpy as jnp
from jax import lax
from jax.experimental import pallas as pl
from jax.experimental.pallas import tpu as pltpu
from jax.sharding import PartitionSpec as P

TILE = 320
CORE, FAR = 1, 2


def grp_swap(value, distance):
    size = lax.axis_size("grp")
    return lax.ppermute(value, "grp", [(k, k ^ distance) for k in range(size)])


def blk_swap(value, mask):
    blocks = lax.axis_size("blk")
    return lax.ppermute(value, "blk", [(b, b ^ mask) for b in range(blocks)])


def far_swap(value):
    blocks, groups = lax.axis_size("blk"), lax.axis_size("grp")
    pairs = [
        (b * groups + k, (b ^ FAR) * groups + groups - 1 - k)
        for b in range(blocks)
        for k in range(groups)
    ]
    return lax.ppermute(value, ("blk", "grp"), pairs)


def plane_hop(value, step):
    stride = 2 * FAR
    masks = range(stride, lax.axis_size("blk"), stride)
    branches = [lambda v, m=m: blk_swap(v, m) for m in masks]
    return lax.switch(step, [lambda v: v] + branches, value)


def tile_kernel(full_width, grad_scale, wit_scale, chunk, first, *refs):
    slots = (len(refs) - 2) // 2
    left = refs[:slots]
    met, proof, *grads = refs[slots:]
    right = [met.at[slot ^ first[0]] for slot in range(slots)]
    gram = jnp.zeros((TILE, met.shape[1]), jnp.float32)
    for slot in range(slots):
        gram += lax.dot_general(
            left[slot][...],
            right[slot][...],
            (((1,), (1,)), ((), ())),
            preferred_element_type=jnp.float32,
        )
    column = lax.broadcasted_iota(jnp.int32, gram.shape, 1)
    sign = jnp.where(column // chunk % 2 == 0, 1.0, -1.0)
    shifted = gram * (1.0 / full_width) + 1.0
    signed = shifted * shifted * sign
    proof[...] = jnp.sum(signed * shifted, axis=1, keepdims=True) * wit_scale
    weight = (3.0 * signed).astype(jnp.bfloat16)
    for slot in range(slots):
        part = jnp.dot(weight, right[slot][...], preferred_element_type=jnp.float32)
        grads[slot][...] = (part * grad_scale).astype(grads[slot].dtype)


def on_device(generated, reference_set, partners):
    block_rows, feat_width = generated.shape
    groups = lax.axis_size("grp")
    full_width = feat_width * groups
    rounds_count = partners.shape[0]
    share = block_rows // groups
    wit_scale = (full_width / (rounds_count * block_rows)) ** 0.5
    grad_scale = 1.0 / (rounds_count * block_rows) ** 0.5
    here = lax.axis_index("grp")

    both = jnp.concatenate(
        [
            generated.reshape(groups, share, feat_width),
            reference_set.reshape(groups, share, feat_width),
        ],
        axis=1,
    )
    own_rows = lax.all_to_all(both, "grp", 0, 0)
    own_rows, generated = lax.optimization_barrier((own_rows, generated))
    far_rows = far_swap(own_rows)
    left = [generated] + [grp_swap(generated, d) for d in range(1, groups)]

    masks = partners[:, 0]
    far_bits = masks // FAR % 2
    order = jnp.where(far_bits[0] > far_bits[1], 1, 0)
    near_count = rounds_count - jnp.sum(far_bits)

    def meet(rows):
        def body(index, met):
            mask = masks[index ^ order]
            sent = lax.cond(
                mask % 2 == CORE, lambda v: blk_swap(v, CORE), lambda v: v, rows
            )
            got = plane_hop(sent, mask // (2 * FAR))
            return lax.dynamic_update_slice(met, got, (0, index * 2 * share, 0))

        return body

    met = jnp.zeros((groups, rounds_count * 2 * share, feat_width), generated.dtype)
    met = lax.fori_loop(0, near_count, meet(own_rows), met)
    met = lax.fori_loop(near_count, rounds_count, meet(far_rows), met)
    first = here.astype(jnp.int32).reshape(1)

    tile = pl.BlockSpec((TILE, feat_width), lambda i: (i, 0))
    out = pl.pallas_call(
        lambda *refs: tile_kernel(full_width, grad_scale, wit_scale, share, *refs),
        grid=(block_rows // TILE,),
        in_specs=[pl.BlockSpec(memory_space=pltpu.SMEM)]
        + [tile] * groups
        + [pl.BlockSpec(met.shape, lambda i: (0, 0, 0))],
        out_specs=[pl.BlockSpec((TILE, 1), lambda i: (i, 0))] + [tile] * groups,
        out_shape=[jax.ShapeDtypeStruct((block_rows, 1), jnp.float32)]
        + [
            jax.ShapeDtypeStruct(
                (block_rows, feat_width), jnp.bfloat16 if d % 2 else jnp.float32
            )
            for d in range(groups)
        ],
        compiler_params=pltpu.CompilerParams(vmem_limit_bytes=40 * 2**20),
    )(first, *left, met)
    mine, near_part, across, across_part = out[1:]
    across = across + grp_swap(across_part, 1).astype(jnp.float32)
    near_part = grp_swap(near_part, 1).astype(jnp.float32)
    across = grp_swap(across.astype(jnp.bfloat16), 2).astype(jnp.float32)
    grads = mine + near_part + across
    proofs = jnp.broadcast_to(out[0].reshape(1, block_rows), (groups, block_rows))
    proof = jnp.sum(lax.all_to_all(proofs, "grp", 0, 0), axis=0)
    return (proof, grads)


def solution(mesh):
    return jax.shard_map(
        on_device,
        mesh=mesh,
        in_specs=(P("blk", "grp"), P("blk", "grp"), P()),
        out_specs=(P("blk"), P("blk", "grp")),
        check_vma=False,
    )
```

time: 288 us -> 200 us (0.69)
  waiting for transfers between devices: 169 us -> 82.7 us
  blocking collectives: 0 us -> 63.7 us
  starting transfers between devices: 70.2 us -> 13.3 us
  other arithmetic: 11.2 us -> 5.32 us
  Pallas kernels: 13.2 us -> 7.5 us
  local copies, waits for them, and re-layouts: 12.1 us -> 17.7 us
    all_to_all x0 -> x2, blocking collectives: none -> 63.7 us  [the longest x1 37.3 us: on_device(): own_rows = lax.all_to_all(both, 'grp', 0, 0)]
    ppermute x8 -> x6, starting transfers between devices: 54 us -> 7.26 us  [grp_swap(): return lax.ppermute(value, 'grp', [(k, k ^ distance) for k in range(size)])]
    ppermute x8 -> x6, waiting for transfers between devices: 48.4 us -> 15.7 us  [grp_swap(): return lax.ppermute(value, 'grp', [(k, k ^ distance) for k in range(size)])]
    all_to_all x1 -> x0, waiting for transfers between devices: 30 us -> none  [on_device(): own_rows = lax.all_to_all(both, 'grp', 0, 0)]
    ppermute x1, waiting for transfers between devices: 31.1 us -> 6.78 us  [far_swap(): return lax.ppermute(value, ('blk', 'grp'), pairs)]
    all_to_all x1 -> x0, starting transfers between devices: 6.03 us -> none  [on_device(): own_rows = lax.all_to_all(both, 'grp', 0, 0)]
    pallas_call x1, Pallas kernels: 13.2 us -> 7.5 us  [on_device(): pl.pallas_call(lambda *refs: tile_kernel(full_width, grad_scale, wit_scal...]
    select_n x2 -> x0, other arithmetic: 5.04 us -> none  [meet(): rows = jnp.where(mask & FAR > 0, far_rows, own_rows)]
  transfers between devices with their start and end apart: 13 -> 9, of which waited for: 7 -> 4; matrix products, arithmetic and copies ran while one was open for 6% -> 9% of each run, Pallas kernels for 0% -> 0%
where the time goes in v1:
time: 200 us; the launch traced here: 198 us
  waiting for transfers between devices  82.7 us (41%)
  blocking collectives  63.7 us (32%)
  local copies, waits for them, and re-layouts  17.7 us (9%)
  starting transfers between devices  13.3 us (7%)
  Pallas kernels  7.5 us (4%)
  other arithmetic  5.32 us (3%)
  loops' own time  4.96 us (2%)
  between operations  2.57 us (1%)
    ppermute x2, waiting for transfers between devices, blk_swap(): return lax.ppermute(value, 'blk', [(b, b ^ mask) for b in range(blocks)])  60.2 us
    all_to_all x1, blocking collectives, on_device(): own_rows = lax.all_to_all(both, 'grp', 0, 0)  37.3 us
    all_to_all x1, blocking collectives, on_device(): proof = jnp.sum(lax.all_to_all(proofs, 'grp', 0, 0), axis=0)  26.4 us
    ppermute x6, waiting for transfers between devices, grp_swap(): return lax.ppermute(value, 'grp', [(k, k ^ distance) for k in range(size)])  15.7 us
    pallas_call x1, Pallas kernels, on_device(): pl.pallas_call(lambda *refs: tile_kernel(full_width, grad_scale, wit_scal...  7.5 us
    ppermute x6, starting transfers between devices, grp_swap(): return lax.ppermute(value, 'grp', [(k, k ^ distance) for k in range(size)])  7.26 us
    cond x4, local copies, waits for them, and re-layouts  7.19 us
    ppermute x1, waiting for transfers between devices, far_swap(): return lax.ppermute(value, ('blk', 'grp'), pairs)  6.78 us
  transfers between devices with their start and end apart: 9, of which 4 were waited for; matrix products, arithmetic and copies ran while one was open for 9% of the time, Pallas kernels for 0%

profile of v1, /device:TPU:6, one launch (start us, length us, event | category | flops | bytes accessed | tf_op | source)
XLA Modules:
  0.0 197.7 jit_solution(15087480167287714696)
XLA Ops:
  2.0 37.3 %all_to_all.11 = bf16[4,320,512]{2,1,0:T(8,128)(2,1)} all-to-all(bf16[4,320,512]{2,1,0:T(8,128)(2,1)S(1)} %pad_maximum_fusion), channel_id=1, replica_groups=mesh['blk'=64,'grp'=4] {'grp'}, dimensions={0} | all-to-all | bytes 2621440 | tf_op jit(solution)/shard_map/all_to_all | solution.py:80
  39.3 3.0 %collective-permute-start.35 = (bf16[4,320,512]{2,1,0:T(8,128)(2,1)}, bf16[4,320,512]{2,1,0:T(8,128)(2,1)}, u32[]{:S(2)}, u32[]{:S(2)}) collective-permute-start(bf16[4,320,512]{2,1,0:T(8,128)(2,1)} %all_to_all.11), channel_id=1, source_target_pairs={{0,11},{1,10},{2,9},{3,8},{4,15},{5,14},{6,13},{7,12},{8,3},{9,2},... | collective-permute-start | bytes 3932168 | tf_op jit(solution)/shard_map/ppermute | solution.py:29
  46.8 1.8 collective-permute-start.33
  48.6 1.5 collective-permute-start.34
  50.0 1.7 broadcast_in_dim.10
  51.7 40.0 %while.24 = (s32[]{:T(128)}, bf16[4,640,512]{2,1,0:T(8,128)(2,1)}, s32[]{:T(128)}, s32[]{:T(128)}, s32[2]{0:T(128)S(1)}, /*index=5*/bf16[4,320,512]{2,1,0:T(8,12...) while((s32[]{:T(128)}, bf16[4,640,512]{2,1,0:T(8,128)(2,1)}, ...), condition=%wide.region_20.21_spmd, body=%wide.region_1.20_spmd.sunk | while | flops 36 | bytes 15729236 | solution.py:102
  54.2 2.5 %conditional.8 = (bf16[4,320,512]{2,1,0:T(8,128)(2,1)}) conditional(s32[]{:T(128)} %convert_element_type.34, bf16[4,320,512]{2,1,0:T(8,128)(2,1)} %get-tuple-element.381, bf16[4,320,512]{2,1,0:T(8,128)(2,1)} %get-tuple-element.381), branch_computations={%region_2.2_spmd, %region_3.3_spmd} | conditional | bytes 5242928 | solution.py:93
  54.2 2.5 %copy.7 = bf16[4,320,512]{2,1,0:T(8,128)(2,1)} copy(bf16[4,320,512]{2,1,0:T(8,128)(2,1)} %param) | data formatting | bytes 2621440 | tf_op jit(solution)/shard_map/while/body/cond
  57.4 31.9 %conditional.9 = (bf16[4,320,512]{2,1,0:T(8,128)(2,1)}) conditional(s32[]{:T(128)} %clamp.14, bf16[4,320,512]{2,1,0:T(8,128)(2,1)} %get-tuple-element.429, bf16[4,320,512]{2,1,0:T(8,128)(2,1)} %get-tuple-element.429, bf16[4,320,512]{2,1,0:T(8,128)(2,1)} %get-tuple-element.429, ...), branch_computations={%region_4.4_spmd, %region_5.5_spmd, %region_6.6_spmd, %region_7.7_... | conditional | bytes 7864368 | solution.py:36
  57.4 1.5 collective-permute-start.8
  58.9 29.2 %collective-permute-done.8 = bf16[4,320,512]{2,1,0:T(8,128)(2,1)S(1)} collective-permute-done((bf16[4,320,512]{2,1,0:T(8,128)(2,1)}, bf16[4,320,512]{2,1,0:T(8,128)(2,1)S(1)}, u32[]{:S(2)}, u32[]{:S(2)}) %collective-permute-start.8) | collective-permute-done | bytes 1310752 | tf_op jit(solution)/shard_map/while/body/cond/branch_8_fun/ppermute | solution.py:19
  89.2 2.5 %constant_dynamic-update-slice_fusion.4 = bf16[4,640,512]{2,1,0:T(8,128)(2,1)} fusion(bf16[4,640,512]{2,1,0:T(8,128)(2,1)} %get-tuple-element.363, bf16[4,320,512]{2,1,0:T(8,128)(2,1)} %get-tuple-element.430, s32[]{:T(128)S(6)} %select_n.98), kind=kLoop, calls=%fused_computation.clone.1 | loop fusion | bytes 2621444 | tf_op jit(solution)/shard_map/while/body/dynamic_update_slice | solution.py:97
  91.7 6.8 %collective-permute-done.35 = bf16[4,320,512]{2,1,0:T(8,128)(2,1)} collective-permute-done((bf16[4,320,512]{2,1,0:T(8,128)(2,1)}, bf16[4,320,512]{2,1,0:T(8,128)(2,1)}, u32[]{:S(2)}, u32[]{:S(2)}) %collective-permute-start.35) | collective-permute-done | bytes 1310752 | tf_op jit(solution)/shard_map/ppermute | solution.py:29
  98.5 41.5 %while.25 = (s32[]{:T(128)}, bf16[4,640,512]{2,1,0:T(8,128)(2,1)}, s32[]{:T(128)}, s32[2]{0:T(128)S(1)}, bf16[4,320,512]{2,1,0:T(8,128)(2,1)}, /*index=5*/s32[]{...) while((s32[]{:T(128)}, bf16[4,640,512]{2,1,0:T(8,128)(2,1)}, ...), condition=%wide.region_40.41_spmd, body=%wide.region_21.40_spmd.sunk | while | flops 36 | bytes 15729228 | solution.py:103
  100.8 2.5 %conditional.10 = (bf16[4,320,512]{2,1,0:T(8,128)(2,1)}) conditional(s32[]{:T(128)} %convert_element_type.35, bf16[4,320,512]{2,1,0:T(8,128)(2,1)} %get-tuple-element.420, bf16[4,320,512]{2,1,0:T(8,128)(2,1)} %get-tuple-element.420), branch_computations={%region_22.22_spmd, %region_23.23_spmd} | conditional | bytes 5242928 | solution.py:93
  100.9 2.5 %copy.26 = bf16[4,320,512]{2,1,0:T(8,128)(2,1)} copy(bf16[4,320,512]{2,1,0:T(8,128)(2,1)} %param.20) | data formatting | bytes 2621440 | tf_op jit(solution)/shard_map/while/body/cond
  103.9 33.6 %conditional.11 = (bf16[4,320,512]{2,1,0:T(8,128)(2,1)}) conditional(s32[]{:T(128)} %clamp.15, bf16[4,320,512]{2,1,0:T(8,128)(2,1)} %get-tuple-element.431, bf16[4,320,512]{2,1,0:T(8,128)(2,1)} %get-tuple-element.431, bf16[4,320,512]{2,1,0:T(8,128)(2,1)} %get-tuple-element.431, ...), branch_computations={%region_24.24_spmd, %region_25.25_spmd, %region_26.26_spmd, %regio... | conditional | bytes 7864368 | solution.py:36
  104.0 1.5 collective-permute-start.24
  105.5 31.0 %collective-permute-done.24 = bf16[4,320,512]{2,1,0:T(8,128)(2,1)S(1)} collective-permute-done((bf16[4,320,512]{2,1,0:T(8,128)(2,1)}, bf16[4,320,512]{2,1,0:T(8,128)(2,1)S(1)}, u32[]{:S(2)}, u32[]{:S(2)}) %collective-permute-start.24) | collective-permute-done | bytes 1310752 | tf_op jit(solution)/shard_map/while/body/cond/branch_8_fun/ppermute | solution.py:19
  137.6 2.5 %constant_dynamic-update-slice_fusion.5 = bf16[4,640,512]{2,1,0:T(8,128)(2,1)} fusion(bf16[4,640,512]{2,1,0:T(8,128)(2,1)} %get-tuple-element.404, bf16[4,320,512]{2,1,0:T(8,128)(2,1)} %get-tuple-element.432, s32[]{:T(128)S(6)} %select_n.102), kind=kLoop, calls=%fused_computation.1.clone.1 | loop fusion | bytes 2621444 | tf_op jit(solution)/shard_map/while/body/dynamic_update_slice | solution.py:97
  142.0 7.5 %shard_map.50 = (f32[640,1]{1,0:T(8,128)S(1)}, f32[640,512]{1,0:T(8,128)S(1)}, bf16[640,512]{1,0:T(8,128)(2,1)}, f32[640,512]{1,0:T(8,128)S(1)}, bf16[640,512]{1,0:T(8,128)(2,1)S(1)}) custom-call(s32[1]{0:T(128)} %bitcast.2.refs_0_, bf16[640,512]{1,0:T(8,128)(2,1)S(1)} %copy-done, bf16[640,512]{1,0:T(8,128)(2,1)S(1)} %collective-permute-done.32.refs_2_, ...), custom_call_target="tpu_custom_call" | custom-call | tf_op jit(solution)/shard_map/pallas_call | solution.py:107
  149.5 2.0 %collective-permute-start.36 = (bf16[640,512]{1,0:T(8,128)(2,1)}, bf16[640,512]{1,0:T(8,128)(2,1)S(1)}, u32[]{:S(2)}, u32[]{:S(2)}) collective-permute-start(bf16[640,512]{1,0:T(8,128)(2,1)} %get-tuple-element.250), channel_id=1, source_target_pairs={{0,1},{1,0},{2,3},{3,2},{4,5},{5,4},{6,7},{7,6},{8,9},{9,8},{10,11... | collective-permute-start | bytes 1966088 | tf_op jit(solution)/shard_map/ppermute | solution.py:14
  151.5 15.6 %collective-permute-done.37 = bf16[640,512]{1,0:T(8,128)(2,1)S(1)} collective-permute-done((bf16[640,512]{1,0:T(8,128)(2,1)S(1)}, bf16[640,512]{1,0:T(8,128)(2,1)S(1)}, u32[]{:S(2)}, u32[]{:S(2)}) %collective-permute-start.37) | collective-permute-done | bytes 655392 | tf_op jit(solution)/shard_map/ppermute | solution.py:14
  169.3 26.4 %all_to_all.12 = f32[4,1,640]{2,1,0:T(1,128)S(1)} all-to-all(f32[4,1,640]{2,1,0:T(1,128)S(1)} %broadcast_in_dim.12), channel_id=1, replica_groups=mesh['blk'=64,'grp'=4] {'grp'}, dimensions={0} | all-to-all | bytes 20480 | tf_op jit(solution)/shard_map/all_to_all | solution.py:129
  (31 shorter events, 13.3 us)
Async XLA Ops:
  2.0 40.3 %copy-start.4 = (s32[2,64]{1,0:T(2,128)S(1)}, s32[2,64]{1,0:T(2,128)}, u32[]{:S(2)}) copy-start(s32[2,64]{1,0:T(2,128)} %param.45) | copy-start | bytes 1540
  2.0 43.5 %copy-start = (bf16[640,512]{1,0:T(8,128)(2,1)S(1)}, bf16[640,512]{1,0:T(8,128)(2,1)}, u32[]{:S(2)}) copy-start(bf16[640,512]{1,0:T(8,128)(2,1)} %refs_1_) | copy-start | bytes 1966084
  39.3 59.2 %collective-permute-start.35 = (bf16[4,320,512]{2,1,0:T(8,128)(2,1)}, bf16[4,320,512]{2,1,0:T(8,128)(2,1)}, u32[]{:S(2)}, u32[]{:S(2)}) collective-permute-start(bf16[4,320,512]{2,1,0:T(8,128)(2,1)} %all_to_all.11), channel_id=1, source_target_pairs={{0,11},{1,10},{2,9},{3,8},{4,15},{5,14},{6,13},{7,12},{8,3},{9,2},... | collective-permute-start | bytes 3932168 | tf_op jit(solution)/shard_map/ppermute | solution.py:29
  45.6 94.5 %collective-permute-start.32 = (bf16[640,512]{1,0:T(8,128)(2,1)S(1)}, bf16[640,512]{1,0:T(8,128)(2,1)S(1)}, u32[]{:S(2)}, u32[]{:S(2)}) collective-permute-start(bf16[640,512]{1,0:T(8,128)(2,1)S(1)} %copy-done), channel_id=1, source_target_pairs={{0,1},{1,0},{2,3},{3,2},{4,5},{5,4},{6,7},{7,6},{8,9},{9,8},{10,11... | collective-permute-start | bytes 1966088 | tf_op jit(solution)/shard_map/ppermute | solution.py:14
  46.8 93.3 %collective-permute-start.33 = (bf16[640,512]{1,0:T(8,128)(2,1)S(1)}, bf16[640,512]{1,0:T(8,128)(2,1)S(1)}, u32[]{:S(2)}, u32[]{:S(2)}) collective-permute-start(bf16[640,512]{1,0:T(8,128)(2,1)S(1)} %copy-done), channel_id=1, source_target_pairs={{0,2},{1,3},{2,0},{3,1},{4,6},{5,7},{6,4},{7,5},{8,10},{9,11},{10,... | collective-permute-start | bytes 1966088 | tf_op jit(solution)/shard_map/ppermute | solution.py:14
  48.6 91.5 %collective-permute-start.34 = (bf16[640,512]{1,0:T(8,128)(2,1)S(1)}, bf16[640,512]{1,0:T(8,128)(2,1)S(1)}, u32[]{:S(2)}, u32[]{:S(2)}) collective-permute-start(bf16[640,512]{1,0:T(8,128)(2,1)S(1)} %copy-done), channel_id=1, source_target_pairs={{0,3},{1,2},{2,1},{3,0},{4,7},{5,6},{6,5},{7,4},{8,11},{9,10},{10,... | collective-permute-start | bytes 1966088 | tf_op jit(solution)/shard_map/ppermute | solution.py:14
  57.4 30.7 %collective-permute-start.8 = (bf16[4,320,512]{2,1,0:T(8,128)(2,1)}, bf16[4,320,512]{2,1,0:T(8,128)(2,1)S(1)}, u32[]{:S(2)}, u32[]{:S(2)}) collective-permute-start(bf16[4,320,512]{2,1,0:T(8,128)(2,1)} %param.10), channel_id=1, source_target_pairs={{0,128},{4,132},{8,136},{12,140},{16,144},{20,148},{24,152},{28,15... | collective-permute-start | bytes 3932168 | tf_op jit(solution)/shard_map/while/body/cond/branch_8_fun/ppermute | solution.py:19
  104.0 32.5 %collective-permute-start.24 = (bf16[4,320,512]{2,1,0:T(8,128)(2,1)}, bf16[4,320,512]{2,1,0:T(8,128)(2,1)S(1)}, u32[]{:S(2)}, u32[]{:S(2)}) collective-permute-start(bf16[4,320,512]{2,1,0:T(8,128)(2,1)} %param.30), channel_id=1, source_target_pairs={{0,128},{4,132},{8,136},{12,140},{16,144},{20,148},{24,152},{28,15... | collective-permute-start | bytes 3932168 | tf_op jit(solution)/shard_map/while/body/cond/branch_8_fun/ppermute | solution.py:19
  140.1 0.8 copy-start.1
  140.9 1.1 copy-start.2
  149.5 17.9 %copy-start.3 = (f32[640,1]{1,0:T(8,128)}, f32[640,1]{1,0:T(8,128)S(1)}, u32[]{:S(2)}) copy-start(f32[640,1]{1,0:T(8,128)S(1)} %get-tuple-element.248) | copy-start | bytes 7684
  149.5 17.7 %collective-permute-start.37 = (bf16[640,512]{1,0:T(8,128)(2,1)S(1)}, bf16[640,512]{1,0:T(8,128)(2,1)S(1)}, u32[]{:S(2)}, u32[]{:S(2)}) collective-permute-start(bf16[640,512]{1,0:T(8,128)(2,1)S(1)} %get-tuple-element.252), channel_id=1, source_target_pairs={{0,1},{1,0},{2,3},{3,2},{4,5},{5,4},{6,7},{7,6},{8,9},{9,8},{10,11... | collective-permute-start | bytes 1966088 | tf_op jit(solution)/shard_map/ppermute | solution.py:14
  149.5 46.8 %collective-permute-start.36 = (bf16[640,512]{1,0:T(8,128)(2,1)}, bf16[640,512]{1,0:T(8,128)(2,1)S(1)}, u32[]{:S(2)}, u32[]{:S(2)}) collective-permute-start(bf16[640,512]{1,0:T(8,128)(2,1)} %get-tuple-element.250), channel_id=1, source_target_pairs={{0,1},{1,0},{2,3},{3,2},{4,5},{5,4},{6,7},{7,6},{8,9},{9,8},{10,11... | collective-permute-start | bytes 1966088 | tf_op jit(solution)/shard_map/ppermute | solution.py:14
  167.4 28.9 %collective-permute-start.38 = (bf16[640,512]{1,0:T(8,128)(2,1)S(1)}, bf16[640,512]{1,0:T(8,128)(2,1)S(1)}, u32[]{:S(2)}, u32[]{:S(2)}) collective-permute-start(bf16[640,512]{1,0:T(8,128)(2,1)S(1)} %add_convert_fusion), channel_id=1, source_target_pairs={{0,2},{1,3},{2,0},{3,1},{4,6},{5,7},{6,4},{7,5},{8,10},{9,11},{10,... | collective-permute-start | bytes 1966088 | tf_op jit(solution)/shard_map/ppermute | solution.py:14

commit v2 on v1

v2 whole, which is shorter than its diff:
```python
import jax
import jax.numpy as jnp
from jax import lax
from jax.experimental import pallas as pl
from jax.experimental.pallas import tpu as pltpu
from jax.sharding import PartitionSpec as P

TILE = 320
CORE, FAR = 1, 2


def grp_swap(value, distance):
    size = lax.axis_size("grp")
    return lax.ppermute(value, "grp", [(k, k ^ distance) for k in range(size)])


def blk_swap(value, mask):
    blocks = lax.axis_size("blk")
    return lax.ppermute(value, "blk", [(b, b ^ mask) for b in range(blocks)])


def far_swap(value):
    blocks, groups = lax.axis_size("blk"), lax.axis_size("grp")
    pairs = [
        (b * groups + k, (b ^ FAR) * groups + groups - 1 - k)
        for b in range(blocks)
        for k in range(groups)
    ]
    return lax.ppermute(value, ("blk", "grp"), pairs)


def plane_hop(value, step):
    stride = 2 * FAR
    masks = range(stride, lax.axis_size("blk"), stride)
    branches = [lambda v, m=m: blk_swap(v, m) for m in masks]
    return lax.switch(step, [lambda v: v] + branches, value)


def weight_kernel(full_width, grad_scale, wit_scale, chunk, first, *refs):
    slots = len(refs) - 4
    left, (met, proof, weight, part) = refs[:slots], refs[slots:]
    gram = jnp.zeros(weight.shape, jnp.float32)
    for slot in range(slots):
        gram += lax.dot_general(
            left[slot][...],
            met[slot ^ first[0]],
            (((1,), (1,)), ((), ())),
            preferred_element_type=jnp.float32,
        )
    column = lax.broadcasted_iota(jnp.int32, gram.shape, 1)
    sign = jnp.where((column // chunk) % 2 == 0, 1.0, -1.0)
    shifted = gram * (1.0 / full_width) + 1.0
    signed = shifted * shifted * sign
    proof[...] = jnp.sum(signed * shifted, axis=1, keepdims=True) * wit_scale
    weight[...] = (3.0 * signed).astype(jnp.bfloat16)
    gradient_part(grad_scale, weight[...], met, slots - 1 ^ first[0], part)


def gradient_part(grad_scale, weight, met, slot, out):
    part = jnp.dot(weight, met[slot], preferred_element_type=jnp.float32)
    out[...] = (part * grad_scale).astype(out.dtype)


def rest_kernel(grad_scale, first, weight, met, *outs):
    for slot, out in enumerate(outs):
        gradient_part(grad_scale, weight[...], met, slot ^ first[0], out)


def untouched(shape, dtype):
    return pl.pallas_call(
        lambda out: None,
        out_specs=pl.BlockSpec(memory_space=pl.ANY),
        out_shape=jax.ShapeDtypeStruct(shape, dtype),
    )()


def on_device(generated, reference_set, partners):
    block_rows, feat_width = generated.shape
    groups = lax.axis_size("grp")
    full_width = feat_width * groups
    rounds_count = partners.shape[0]
    share = block_rows // groups
    wit_scale = (full_width / (rounds_count * block_rows)) ** 0.5
    grad_scale = 1.0 / (rounds_count * block_rows) ** 0.5
    here = lax.axis_index("grp")

    both = jnp.concatenate(
        [
            generated.reshape(groups, share, feat_width),
            reference_set.reshape(groups, share, feat_width),
        ],
        axis=1,
    )
    masks = [partners[r, 0] for r in range(rounds_count)]
    far_bits = [(m >> 1) & 1 for m in masks]
    swapped = far_bits[0] > far_bits[1]
    masks = [
        jnp.where(swapped, masks[1], masks[0]),
        jnp.where(swapped, masks[0], masks[1]),
    ]
    near_count = rounds_count - far_bits[0] - far_bits[1]
    met = untouched((groups, rounds_count * 2 * share, feat_width), generated.dtype)
    first = here.astype(jnp.int32).reshape(1)
    own_rows = lax.all_to_all(both, "grp", 0, 0)
    own_rows, generated = lax.optimization_barrier((own_rows, generated))
    far_rows = far_swap(own_rows)
    left = [generated] + [grp_swap(generated, d) for d in range(1, groups)]

    def put(met, got, index):
        return lax.dynamic_update_slice(met, got, (0, index * 2 * share, 0))

    def meet(rows):
        def body(index, carry):
            met, mask, later = carry
            got = plane_hop(rows, mask >> 2)
            met = lax.cond(
                (mask & CORE) > 0,
                lambda m, g, i: put(m, blk_swap(g, CORE), i),
                put,
                met,
                got,
                index,
            )
            return met, later, later

        return body

    carry = (met, *masks)
    carry = lax.fori_loop(0, near_count, meet(own_rows), carry)
    met, _, _ = lax.fori_loop(near_count, rounds_count, meet(far_rows), carry)

    def tiled(width):
        return pl.BlockSpec((TILE, width), lambda i: (i, 0))

    def shaped(width, dtype):
        return jax.ShapeDtypeStruct((block_rows, width), dtype)

    scalar = pl.BlockSpec(memory_space=pltpu.SMEM)
    whole = pl.BlockSpec(met.shape, lambda i: (0, 0, 0))
    params = pltpu.CompilerParams(vmem_limit_bytes=40 * 2**20)
    columns = met.shape[1]
    proof, weight, across_part = pl.pallas_call(
        lambda *refs: weight_kernel(full_width, grad_scale, wit_scale, share, *refs),
        grid=(block_rows // TILE,),
        in_specs=[scalar] + [tiled(feat_width)] * groups + [whole],
        out_specs=[tiled(1), tiled(columns), tiled(feat_width)],
        out_shape=[
            shaped(1, jnp.float32),
            shaped(columns, jnp.bfloat16),
            shaped(feat_width, jnp.bfloat16),
        ],
        compiler_params=params,
    )(first, *left, met)
    cut = block_rows * 2 // 5
    spans = (slice(0, cut), slice(cut, block_rows))
    halves = [grp_swap(across_part[span], 1) for span in spans]
    mine, near_part, across = pl.pallas_call(
        lambda *refs: rest_kernel(grad_scale, *refs),
        grid=(block_rows // TILE,),
        in_specs=[scalar, tiled(columns), whole],
        out_specs=[tiled(feat_width)] * 3,
        out_shape=[
            shaped(feat_width, jnp.float32),
            shaped(feat_width, jnp.bfloat16),
            shaped(feat_width, jnp.float32),
        ],
        compiler_params=params,
    )(first, weight, met)
    crossed = []
    for span, got in zip(spans, halves):
        total = across[span] + got.astype(jnp.float32)
        crossed.append(grp_swap(total.astype(jnp.bfloat16), 2))
    near_part = grp_swap(near_part, 1).astype(jnp.float32)
    across = jnp.concatenate(crossed).astype(jnp.float32)
    grads = mine + near_part + across
    proofs = jnp.broadcast_to(proof.reshape(1, block_rows), (groups, block_rows))
    proof = jnp.sum(lax.all_to_all(proofs, "grp", 0, 0), axis=0)
    return (proof, grads)


def solution(mesh):
    return jax.shard_map(
        on_device,
        mesh=mesh,
        in_specs=(P("blk", "grp"), P("blk", "grp"), P()),
        out_specs=(P("blk"), P("blk", "grp")),
        check_vma=False,
    )
```

time: 200 us -> 191 us (0.955); the launches traced: 198 us -> 192 us
  waiting for transfers between devices: 82.7 us -> 96.1 us
  local copies, waits for them, and re-layouts: 17.7 us -> 5.53 us
  blocking collectives: 63.7 us -> 57.2 us
  loops' own time: 4.96 us -> 0.07 us
  between operations: 2.57 us -> 4.64 us
    ppermute x1, waiting for transfers between devices: 6.78 us -> 14.3 us  [far_swap(): return lax.ppermute(value, ('blk', 'grp'), pairs)]
    cond x4 -> x0, local copies, waits for them, and re-layouts: 7.19 us -> none
    all_to_all x1, blocking collectives: 26.4 us -> 19.9 us  [on_device(): proof = jnp.sum(lax.all_to_all(proofs, 'grp', 0, 0), axis=0)]
    ppermute x6 -> x8, waiting for transfers between devices: 15.7 us -> 21.1 us  [grp_swap(): return lax.ppermute(value, 'grp', [(k, k ^ distance) for k in range(size)])]
    another operation x4, loops' own time: 4.89 us -> 0.03 us  [the longest x1 0.03 us: on_device(): carry = lax.fori_loop(0, near_count, meet(own_rows), carry)]
    ppermute x6 -> x8, starting transfers between devices: 7.26 us -> 7.69 us  [grp_swap(): return lax.ppermute(value, 'grp', [(k, k ^ distance) for k in range(size)])]
    pallas_call x1 -> x3, Pallas kernels: 7.5 us -> 7.61 us  [the longest x1 5.71 us: on_device(): pl.pallas_call(lambda *refs: weight_kernel(full_width, grad_scale, wit_sc...]
  transfers between devices with their start and end apart: 9 -> 11, of which waited for: 4 -> 5; matrix products, arithmetic and copies ran while one was open for 9% -> 4% of each run, Pallas kernels for 0% -> 1%
where the time goes in v2:
time: 191 us; the launch traced here: 192 us
  waiting for transfers between devices  96.1 us (50%)
  blocking collectives  57.2 us (30%)
  starting transfers between devices  15.2 us (8%)
  Pallas kernels  7.61 us (4%)
  local copies, waits for them, and re-layouts  5.53 us (3%)
  other arithmetic  5.44 us (3%)
  between operations  4.64 us (2%)
    ppermute x2, waiting for transfers between devices, blk_swap(): return lax.ppermute(value, 'blk', [(b, b ^ mask) for b in range(blocks)])  60.8 us
    all_to_all x1, blocking collectives, on_device(): own_rows = lax.all_to_all(both, 'grp', 0, 0)  37.3 us
    ppermute x8, waiting for transfers between devices, grp_swap(): return lax.ppermute(value, 'grp', [(k, k ^ distance) for k in range(size)])  21.1 us
    all_to_all x1, blocking collectives, on_device(): proof = jnp.sum(lax.all_to_all(proofs, 'grp', 0, 0), axis=0)  19.9 us
    ppermute x1, waiting for transfers between devices, far_swap(): return lax.ppermute(value, ('blk', 'grp'), pairs)  14.3 us
    ppermute x8, starting transfers between devices, grp_swap(): return lax.ppermute(value, 'grp', [(k, k ^ distance) for k in range(size)])  7.69 us
    pallas_call x1, Pallas kernels, on_device(): pl.pallas_call(lambda *refs: weight_kernel(full_width, grad_scale, wit_sc...  5.71 us
    dynamic_update_slice x2, local copies, waits for them, and re-layouts, put(): return lax.dynamic_update_slice(met, got, (0, index * 2 * share, 0))  4.94 us
  transfers between devices with their start and end apart: 11, of which 5 were waited for; matrix products, arithmetic and copies ran while one was open for 4% of the time, Pallas kernels for 1%

profile of v2, /device:TPU:6, one launch (start us, length us, event | category | flops | bytes accessed | tf_op | source)
XLA Modules:
  0.0 191.7 jit_solution(7377321824283213111)
XLA Ops:
  0.6 1.4 pad_maximum_fusion
  2.0 37.3 %all_to_all.11 = bf16[4,320,512]{2,1,0:T(8,128)(2,1)} all-to-all(bf16[4,320,512]{2,1,0:T(8,128)(2,1)S(1)} %pad_maximum_fusion), channel_id=1, replica_groups=mesh['blk'=64,'grp'=4] {'grp'}, dimensions={0} | all-to-all | bytes 2621440 | tf_op jit(solution)/shard_map/all_to_all | solution.py:104
  39.3 3.1 %collective-permute-start.35 = (bf16[4,320,512]{2,1,0:T(8,128)(2,1)}, bf16[4,320,512]{2,1,0:T(8,128)(2,1)}, u32[]{:S(2)}, u32[]{:S(2)}) collective-permute-start(bf16[4,320,512]{2,1,0:T(8,128)(2,1)} %all_to_all.11), channel_id=1, source_target_pairs={{0,11},{1,10},{2,9},{3,8},{4,15},{5,14},{6,13},{7,12},{8,3},{9,2},... | collective-permute-start | bytes 3932168 | tf_op jit(solution)/shard_map/ppermute | solution.py:29
  43.5 1.8 collective-permute-start.33
  45.3 1.5 collective-permute-start.34
  51.2 33.1 %while.24 = (s32[]{:T(128)}, bf16[4,640,512]{2,1,0:T(8,128)(2,1)}, s32[]{:T(128)}, s32[]{:T(128)}, bf16[4,320,512]{2,1,0:T(8,128)(2,1)}, /*index=5*/s32[]{:T(128)}, s32[]{:T(128)}, s32[]{:T(128)}, s32[]{:T(128)}, s32[]{:T(128)}) while((s32[]{:T(128)}, bf16[4,640,512]{2,1,0:T(8,128)(2,1)}, s32[]{:T(128)}, s32[]{:T(128)}, ...), condition=%wide.region_19.20_spmd, body=%wide.region_0.19_spmd.sunk | while | flops 11 | bytes 13107557 | solution.py:129
  51.2 30.6 %conditional.8 = (bf16[4,320,512]{2,1,0:T(8,128)(2,1)}) conditional(s32[]{:T(128)} %clamp.8, bf16[4,320,512]{2,1,0:T(8,128)(2,1)} %get-tuple-element.307, bf16[4,320,512]{2,1,0:T(8,128)(2,1)} %get-tuple-element.307, bf16[4,320,512]{2,1,0:T(8,128)(2,1)} %get-tuple-element.307, ...), branch_computations={%region_1.1_spmd, %region_2.2_spmd, %region_3.3_spmd, %region_4.4_... | conditional | bytes 5242928 | solution.py:36
  51.8 30.0 %collective-permute-done.11 = bf16[4,320,512]{2,1,0:T(8,128)(2,1)} collective-permute-done((bf16[4,320,512]{2,1,0:T(8,128)(2,1)}, bf16[4,320,512]{2,1,0:T(8,128)(2,1)}, u32[]{:S(2)}, u32[]{:S(2)}) %collective-permute-start.11) | collective-permute-done | bytes 1310752 | tf_op jit(solution)/shard_map/while/body/cond/branch_12_fun/ppermute | solution.py:19
  81.8 2.5 %conditional.9 = (bf16[4,640,512]{2,1,0:T(8,128)(2,1)}) conditional(s32[]{:T(128)} %convert_element_type.38, (s32[]{:T(128)}, bf16[4,640,512]{2,1,0:T(8,128)(2,1)}, bf16[4,320,512]{2,1,0:T(8,128)(2,1)}) %tuple.149, (bf16[4,320,512]{2,1,0:T(8,128)(2,1)}, s32[]{:T(128)}, bf16[4,640,512]{2,1,0:T(8,128)(2,1)}) %tuple.150), branch_computations={%region_17.17_spmd, %region_18.18_spmd} | conditional | flops 4 | bytes 7864418 | solution.py:116
  81.8 2.5 %constant_dynamic-update-slice_fusion = bf16[4,640,512]{2,1,0:T(8,128)(2,1)} fusion(bf16[4,640,512]{2,1,0:T(8,128)(2,1)} %get-tuple-element.140, bf16[4,320,512]{2,1,0:T(8,128)(2,1)} %get-tuple-element.141, s32[]{:T(128)S(6)} %select_n.13), kind=kLoop, calls=%fused_computation | loop fusion | bytes 2621444 | tf_op jit(solution)/shard_map/while/body/cond/branch_0_fun/dynamic_update_slice | solution.py:110
  84.3 14.3 %collective-permute-done.35 = bf16[4,320,512]{2,1,0:T(8,128)(2,1)} collective-permute-done((bf16[4,320,512]{2,1,0:T(8,128)(2,1)}, bf16[4,320,512]{2,1,0:T(8,128)(2,1)}, u32[]{:S(2)}, u32[]{:S(2)}) %collective-permute-start.35) | collective-permute-done | bytes 1310752 | tf_op jit(solution)/shard_map/ppermute | solution.py:29
  98.5 37.1 %while.25 = (s32[]{:T(128)}, bf16[4,640,512]{2,1,0:T(8,128)(2,1)}, s32[]{:T(128)}, bf16[4,320,512]{2,1,0:T(8,128)(2,1)}, s32[]{:T(128)}, /*index=5*/s32[]{:T(128)}, s32[]{:T(128)}, s32[]{:T(128)}, s32[]{:T(128)}) while((s32[]{:T(128)}, bf16[4,640,512]{2,1,0:T(8,128)(2,1)}, s32[]{:T(128)}, bf16[4,320,512]{2,1,0:T(8,128)(2,1)}, s32[]{:T(128)}, ...), condition=%wide.region_39.40_spmd, body=%wide.region_20.39_spmd.sunk | while | flops 11 | bytes 13107549 | solution.py:130
  98.5 34.6 %conditional.10 = (bf16[4,320,512]{2,1,0:T(8,128)(2,1)}) conditional(s32[]{:T(128)} %clamp.9, bf16[4,320,512]{2,1,0:T(8,128)(2,1)} %get-tuple-element.334, bf16[4,320,512]{2,1,0:T(8,128)(2,1)} %get-tuple-element.334, bf16[4,320,512]{2,1,0:T(8,128)(2,1)} %get-tuple-element.334, ...), branch_computations={%region_21.21_spmd, %region_22.22_spmd, %region_23.23_spmd, %regio... | conditional | bytes 5242928 | solution.py:36
  98.5 3.9 %collective-permute-start.25 = (bf16[4,320,512]{2,1,0:T(8,128)(2,1)}, bf16[4,320,512]{2,1,0:T(8,128)(2,1)}, u32[]{:S(2)}, u32[]{:S(2)}) collective-permute-start(bf16[4,320,512]{2,1,0:T(8,128)(2,1)} %param.31), channel_id=1, source_target_pairs={{0,176},{4,180},{8,184},{12,188},{16,160},{20,164},{24,168},{28,17... | collective-permute-start | bytes 3932168 | tf_op jit(solution)/shard_map/while/body/cond/branch_11_fun/ppermute | solution.py:19
  102.4 30.8 %collective-permute-done.25 = bf16[4,320,512]{2,1,0:T(8,128)(2,1)} collective-permute-done((bf16[4,320,512]{2,1,0:T(8,128)(2,1)}, bf16[4,320,512]{2,1,0:T(8,128)(2,1)}, u32[]{:S(2)}, u32[]{:S(2)}) %collective-permute-start.25) | collective-permute-done | bytes 1310752 | tf_op jit(solution)/shard_map/while/body/cond/branch_11_fun/ppermute | solution.py:19
  133.1 2.5 %conditional.11 = (bf16[4,640,512]{2,1,0:T(8,128)(2,1)}) conditional(s32[]{:T(128)} %convert_element_type.39, (s32[]{:T(128)}, bf16[4,640,512]{2,1,0:T(8,128)(2,1)}, bf16[4,320,512]{2,1,0:T(8,128)(2,1)}) %tuple.152, (bf16[4,320,512]{2,1,0:T(8,128)(2,1)}, s32[]{:T(128)}, bf16[4,640,512]{2,1,0:T(8,128)(2,1)}) %tuple.153), branch_computations={%region_37.37_spmd, %region_38.38_spmd} | conditional | flops 4 | bytes 7864418 | solution.py:116
  133.1 2.5 %constant_dynamic-update-slice_fusion.2 = bf16[4,640,512]{2,1,0:T(8,128)(2,1)} fusion(bf16[4,640,512]{2,1,0:T(8,128)(2,1)} %get-tuple-element.154, bf16[4,320,512]{2,1,0:T(8,128)(2,1)} %get-tuple-element.155, s32[]{:T(128)S(6)} %select_n.15), kind=kLoop, calls=%fused_computation.2 | loop fusion | bytes 2621444 | tf_op jit(solution)/shard_map/while/body/cond/branch_0_fun/dynamic_update_slice | solution.py:110
  135.6 5.7 %shard_map.51 = (f32[640,1]{1,0:T(8,128)S(1)}, bf16[640,640]{1,0:T(8,128)(2,1)S(1)}, bf16[640,512]{1,0:T(8,128)(2,1)S(1)}) custom-call(s32[1]{0:T(128)} %bitcast.refs_0_, bf16[640,512]{1,0:T(8,128)(2,1)S(1)} %copy-done, bf16[640,512]{1,0:T(8,128)(2,1)S(1)} %collective-permute-done.32.refs_2_, bf16[640,512]{1,0:T(8,128)(2,1)S(1)} %collective-permute-done.33.refs_3_, ...), custom_call_target="tpu_custom_call" | custom-call | tf_op jit(solution)/shard_map/pallas_call | solution.py:142
  141.5 1.9 shard_map.52
  143.4 2.1 %collective-permute-start.37 = (bf16[256,512]{1,0:T(8,128)(2,1)S(1)}, bf16[256,512]{1,0:T(8,128)(2,1)S(1)}, u32[]{:S(2)}, u32[]{:S(2)}) collective-permute-start(bf16[256,512]{1,0:T(8,128)(2,1)S(1)} %slice.21), channel_id=1, source_target_pairs={{0,1},{1,0},{2,3},{3,2},{4,5},{5,4},{6,7},{7,6},{8,9},{9,8},{10,11... | collective-permute-start | bytes 786440 | tf_op jit(solution)/shard_map/ppermute | solution.py:14
  145.6 7.9 %collective-permute-done.39 = bf16[384,512]{1,0:T(8,128)(2,1)S(1)} collective-permute-done((bf16[384,512]{1,0:T(8,128)(2,1)S(1)}, bf16[384,512]{1,0:T(8,128)(2,1)S(1)}, u32[]{:S(2)}, u32[]{:S(2)}) %collective-permute-start.39) | collective-permute-done | bytes 393248 | tf_op jit(solution)/shard_map/ppermute | solution.py:14
  154.4 13.1 %collective-permute-done.37 = bf16[256,512]{1,0:T(8,128)(2,1)S(1)} collective-permute-done((bf16[256,512]{1,0:T(8,128)(2,1)S(1)}, bf16[256,512]{1,0:T(8,128)(2,1)S(1)}, u32[]{:S(2)}, u32[]{:S(2)}) %collective-permute-start.37) | collective-permute-done | bytes 262176 | tf_op jit(solution)/shard_map/ppermute | solution.py:14
  168.8 19.9 %all_to_all.12 = f32[4,1,640]{2,1,0:T(1,128)S(1)} all-to-all(f32[4,1,640]{2,1,0:T(1,128)S(1)} %broadcast_in_dim.8), channel_id=1, replica_groups=mesh['blk'=64,'grp'=4] {'grp'}, dimensions={0} | all-to-all | bytes 20480 | tf_op jit(solution)/shard_map/all_to_all | solution.py:177
  189.3 2.4 %convert_add_fusion = f32[640,512]{1,0:T(8,128)} fusion(f32[640,512]{1,0:T(8,128)S(1)} %get-tuple-element.186, bf16[640,512]{1,0:T(8,128)(2,1)S(1)} %collective-permute-done.36, bf16[384,512]{1,0:T(8,128)(2,1)} %collective-permute-done.40, bf16[256,512]{1,0:T(8,128)(2,1)} %collective-permute-done.38), kind=kLoop, calls=%fused_computation.5 | loop fusion | flops 2293760 | bytes 3932160 | tf_op jit(solution)/shard_map/add | solution.py:175
  (27 shorter events, 5.2 us)
Async XLA Ops:
  2.0 40.4 %copy-start = (bf16[640,512]{1,0:T(8,128)(2,1)S(1)}, bf16[640,512]{1,0:T(8,128)(2,1)}, u32[]{:S(2)}) copy-start(bf16[640,512]{1,0:T(8,128)(2,1)} %refs_1_) | copy-start | bytes 1966084
  2.0 44.7 %copy-start.2 = (s32[2,64]{1,0:T(2,128)S(1)}, s32[2,64]{1,0:T(2,128)}, u32[]{:S(2)}) copy-start(s32[2,64]{1,0:T(2,128)} %param.45) | copy-start | bytes 1540
  39.3 59.2 %collective-permute-start.35 = (bf16[4,320,512]{2,1,0:T(8,128)(2,1)}, bf16[4,320,512]{2,1,0:T(8,128)(2,1)}, u32[]{:S(2)}, u32[]{:S(2)}) collective-permute-start(bf16[4,320,512]{2,1,0:T(8,128)(2,1)} %all_to_all.11), channel_id=1, source_target_pairs={{0,11},{1,10},{2,9},{3,8},{4,15},{5,14},{6,13},{7,12},{8,3},{9,2},... | collective-permute-start | bytes 3932168 | tf_op jit(solution)/shard_map/ppermute | solution.py:29
  42.4 93.3 %collective-permute-start.32 = (bf16[640,512]{1,0:T(8,128)(2,1)S(1)}, bf16[640,512]{1,0:T(8,128)(2,1)S(1)}, u32[]{:S(2)}, u32[]{:S(2)}) collective-permute-start(bf16[640,512]{1,0:T(8,128)(2,1)S(1)} %copy-done), channel_id=1, source_target_pairs={{0,1},{1,0},{2,3},{3,2},{4,5},{5,4},{6,7},{7,6},{8,9},{9,8},{10,11... | collective-permute-start | bytes 1966088 | tf_op jit(solution)/shard_map/ppermute | solution.py:14
  43.5 92.2 %collective-permute-start.33 = (bf16[640,512]{1,0:T(8,128)(2,1)S(1)}, bf16[640,512]{1,0:T(8,128)(2,1)S(1)}, u32[]{:S(2)}, u32[]{:S(2)}) collective-permute-start(bf16[640,512]{1,0:T(8,128)(2,1)S(1)} %copy-done), channel_id=1, source_target_pairs={{0,2},{1,3},{2,0},{3,1},{4,6},{5,7},{6,4},{7,5},{8,10},{9,11},{10,... | collective-permute-start | bytes 1966088 | tf_op jit(solution)/shard_map/ppermute | solution.py:14
  45.3 90.3 %collective-permute-start.34 = (bf16[640,512]{1,0:T(8,128)(2,1)S(1)}, bf16[640,512]{1,0:T(8,128)(2,1)S(1)}, u32[]{:S(2)}, u32[]{:S(2)}) collective-permute-start(bf16[640,512]{1,0:T(8,128)(2,1)S(1)} %copy-done), channel_id=1, source_target_pairs={{0,3},{1,2},{2,1},{3,0},{4,7},{5,6},{6,5},{7,4},{8,11},{9,10},{10,... | collective-permute-start | bytes 1966088 | tf_op jit(solution)/shard_map/ppermute | solution.py:14
  51.2 30.5 %collective-permute-start.11 = (bf16[4,320,512]{2,1,0:T(8,128)(2,1)}, bf16[4,320,512]{2,1,0:T(8,128)(2,1)}, u32[]{:S(2)}, u32[]{:S(2)}) collective-permute-start(bf16[4,320,512]{2,1,0:T(8,128)(2,1)} %param.12), channel_id=1, source_target_pairs={{0,192},{4,196},{8,200},{12,204},{16,208},{20,212},{24,216},{28,22... | collective-permute-start | bytes 3932168 | tf_op jit(solution)/shard_map/while/body/cond/branch_12_fun/ppermute | solution.py:19
  98.5 34.6 %collective-permute-start.25 = (bf16[4,320,512]{2,1,0:T(8,128)(2,1)}, bf16[4,320,512]{2,1,0:T(8,128)(2,1)}, u32[]{:S(2)}, u32[]{:S(2)}) collective-permute-start(bf16[4,320,512]{2,1,0:T(8,128)(2,1)} %param.31), channel_id=1, source_target_pairs={{0,176},{4,180},{8,184},{12,188},{16,160},{20,164},{24,168},{28,17... | collective-permute-start | bytes 3932168 | tf_op jit(solution)/shard_map/while/body/cond/branch_11_fun/ppermute | solution.py:19
  135.6 5.9 %copy-start.1 = (bf16[4,640,512]{2,1,0:T(8,128)(2,1)S(1)}, bf16[4,640,512]{2,1,0:T(8,128)(2,1)}, u32[]{:S(2)}) copy-start(bf16[4,640,512]{2,1,0:T(8,128)(2,1)} %get-tuple-element.183.refs_5_.refs_2_) | copy-start | bytes 7864324
  141.4 12.1 %collective-permute-start.39 = (bf16[384,512]{1,0:T(8,128)(2,1)S(1)}, bf16[384,512]{1,0:T(8,128)(2,1)S(1)}, u32[]{:S(2)}, u32[]{:S(2)}) collective-permute-start(bf16[384,512]{1,0:T(8,128)(2,1)S(1)} %slice.23), channel_id=1, source_target_pairs={{0,1},{1,0},{2,3},{3,2},{4,5},{5,4},{6,7},{7,6},{8,9},{9,8},{10,11... | collective-permute-start | bytes 1179656 | tf_op jit(solution)/shard_map/ppermute | solution.py:14
  143.4 24.1 %collective-permute-start.37 = (bf16[256,512]{1,0:T(8,128)(2,1)S(1)}, bf16[256,512]{1,0:T(8,128)(2,1)S(1)}, u32[]{:S(2)}, u32[]{:S(2)}) collective-permute-start(bf16[256,512]{1,0:T(8,128)(2,1)S(1)} %slice.21), channel_id=1, source_target_pairs={{0,1},{1,0},{2,3},{3,2},{4,5},{5,4},{6,7},{7,6},{8,9},{9,8},{10,11... | collective-permute-start | bytes 786440 | tf_op jit(solution)/shard_map/ppermute | solution.py:14
  145.5 43.7 %collective-permute-start.36 = (bf16[640,512]{1,0:T(8,128)(2,1)S(1)}, bf16[640,512]{1,0:T(8,128)(2,1)S(1)}, u32[]{:S(2)}, u32[]{:S(2)}) collective-permute-start(bf16[640,512]{1,0:T(8,128)(2,1)S(1)} %get-tuple-element.187), channel_id=1, source_target_pairs={{0,1},{1,0},{2,3},{3,2},{4,5},{5,4},{6,7},{7,6},{8,9},{9,8},{10,11... | collective-permute-start | bytes 1966088 | tf_op jit(solution)/shard_map/ppermute | solution.py:14
  153.7 35.6 %collective-permute-start.40 = (bf16[384,512]{1,0:T(8,128)(2,1)S(1)}, bf16[384,512]{1,0:T(8,128)(2,1)}, u32[]{:S(2)}, u32[]{:S(2)}) collective-permute-start(bf16[384,512]{1,0:T(8,128)(2,1)S(1)} %add_convert_fusion), channel_id=1, source_target_pairs={{0,2},{1,3},{2,0},{3,1},{4,6},{5,7},{6,4},{7,5},{8,10},{9,11},{10,... | collective-permute-start | bytes 1179656 | tf_op jit(solution)/shard_map/ppermute | solution.py:14
  168.3 20.9 %collective-permute-start.38 = (bf16[256,512]{1,0:T(8,128)(2,1)}, bf16[256,512]{1,0:T(8,128)(2,1)}, u32[]{:S(2)}, u32[]{:S(2)}) collective-permute-start(bf16[256,512]{1,0:T(8,128)(2,1)} %add_convert_fusion.1), channel_id=1, source_target_pairs={{0,2},{1,3},{2,0},{3,1},{4,6},{5,7},{6,4},{7,5},{8,10},{9,11},{10,... | collective-permute-start | bytes 786440 | tf_op jit(solution)/shard_map/ppermute | solution.py:14

commit v3 on v2

--- a/solution.py
+++ b/solution.py
@@ -36,14 +36,14 @@
     return lax.switch(step, [lambda v: v] + branches, value)
 
 
-def weight_kernel(full_width, grad_scale, wit_scale, chunk, first, *refs):
-    slots = len(refs) - 4
-    left, (met, proof, weight, part) = refs[:slots], refs[slots:]
+def weight_kernel(full_width, grad_scale, wit_scale, chunk, *refs):
+    slots = len(refs) - 5
+    left, (met, proof, weight, *parts) = refs[:slots], refs[slots:]
     gram = jnp.zeros(weight.shape, jnp.float32)
     for slot in range(slots):
         gram += lax.dot_general(
             left[slot][...],
-            met[slot ^ first[0]],
+            met[slot],
             (((1,), (1,)), ((), ())),
             preferred_element_type=jnp.float32,
         )
@@ -53,7 +53,11 @@
     signed = shifted * shifted * sign
     proof[...] = jnp.sum(signed * shifted, axis=1, keepdims=True) * wit_scale
     weight[...] = (3.0 * signed).astype(jnp.bfloat16)
-    gradient_part(grad_scale, weight[...], met, slots - 1 ^ first[0], part)
+    for step, part in enumerate(parts):
+
+        @pl.when(pl.program_id(0) == step)
+        def _(part=part):
+            gradient_part(grad_scale, weight[...], met, slots - 1, part)
 
 
 def gradient_part(grad_scale, weight, met, slot, out):
@@ -61,9 +65,24 @@
     out[...] = (part * grad_scale).astype(out.dtype)
 
 
-def rest_kernel(grad_scale, first, weight, met, *outs):
+def rest_kernel(grad_scale, weight, met, *outs):
     for slot, out in enumerate(outs):
-        gradient_part(grad_scale, weight[...], met, slot ^ first[0], out)
+        gradient_part(grad_scale, weight[...], met, slot, out)
+
+
+def total_kernel(grad_scale, slot, weight, met, got, out):
+    part = jnp.dot(weight[...], met[slot], preferred_element_type=jnp.float32)
+    out[...] = (part * grad_scale + got[...].astype(jnp.float32)).astype(out.dtype)
+
+
+def final_kernel(mine, near, *refs):
+    *crossed, out = refs
+    for step, across in enumerate(crossed):
+
+        @pl.when(pl.program_id(0) == step)
+        def _(across=across):
+            near_sum = mine[...] + near[...].astype(jnp.float32)
+            out[...] = near_sum + across[...].astype(jnp.float32)
 
 
 def untouched(shape, dtype):
@@ -84,13 +103,20 @@
     grad_scale = 1.0 / (rounds_count * block_rows) ** 0.5
     here = lax.axis_index("grp")
 
-    both = jnp.concatenate(
-        [
-            generated.reshape(groups, share, feat_width),
-            reference_set.reshape(groups, share, feat_width),
-        ],
-        axis=1,
-    )
+    def chunk_for(member):
+        return jnp.concatenate(
+            [
+                lax.dynamic_slice_in_dim(x, member * share, share)
+                for x in (generated, reference_set)
+            ]
+        )
+
+    pieces = [chunk_for(here)]
+    for distance in range(1, groups):
+        pieces.append(grp_swap(chunk_for(here ^ distance), distance))
+    late = far_swap(jnp.stack(pieces[:1:-1]))
+    early = far_swap(jnp.stack(pieces[1::-1]))
+    own_rows = jnp.stack(pieces)
     masks = [partners[r, 0] for r in range(rounds_count)]
     far_bits = [(m >> 1) & 1 for m in masks]
     swapped = far_bits[0] > far_bits[1]
@@ -100,10 +126,9 @@
     ]
     near_count = rounds_count - far_bits[0] - far_bits[1]
     met = untouched((groups, rounds_count * 2 * share, feat_width), generated.dtype)
-    first = here.astype(jnp.int32).reshape(1)
-    own_rows = lax.all_to_all(both, "grp", 0, 0)
-    own_rows, generated = lax.optimization_barrier((own_rows, generated))
-    far_rows = far_swap(own_rows)
+    own_rows, generated, masks, near_count, met = lax.optimization_barrier(
+        (own_rows, generated, masks, near_count, met)
+    )
     left = [generated] + [grp_swap(generated, d) for d in range(1, groups)]
 
     def put(met, got, index):
@@ -127,6 +152,8 @@
 
     carry = (met, *masks)
     carry = lax.fori_loop(0, near_count, meet(own_rows), carry)
+    carry, late, early = lax.optimization_barrier((carry, late, early))
+    far_rows = jnp.concatenate([late, early])
     met, _, _ = lax.fori_loop(near_count, rounds_count, meet(far_rows), carry)
 
     def tiled(width):
@@ -135,44 +162,52 @@
     def shaped(width, dtype):
         return jax.ShapeDtypeStruct((block_rows, width), dtype)
 
-    scalar = pl.BlockSpec(memory_space=pltpu.SMEM)
+    once = pl.BlockSpec((TILE, feat_width), lambda i: (0, 0))
     whole = pl.BlockSpec(met.shape, lambda i: (0, 0, 0))
     params = pltpu.CompilerParams(vmem_limit_bytes=40 * 2**20)
     columns = met.shape[1]
-    proof, weight, across_part = pl.pallas_call(
+    proof, weight, *across_parts = pl.pallas_call(
         lambda *refs: weight_kernel(full_width, grad_scale, wit_scale, share, *refs),
         grid=(block_rows // TILE,),
-        in_specs=[scalar] + [tiled(feat_width)] * groups + [whole],
-        out_specs=[tiled(1), tiled(columns), tiled(feat_width)],
-        out_shape=[
-            shaped(1, jnp.float32),
-            shaped(columns, jnp.bfloat16),
-            shaped(feat_width, jnp.bfloat16),
-        ],
+        in_specs=[tiled(feat_width)] * groups + [whole],
+        out_specs=[tiled(1), tiled(columns)] + [once] * 2,
+        out_shape=[shaped(1, jnp.float32), shaped(columns, jnp.bfloat16)]
+        + [jax.ShapeDtypeStruct((TILE, feat_width), jnp.bfloat16)] * 2,
         compiler_params=params,
-    )(first, *left, met)
-    cut = block_rows * 2 // 5
-    spans = (slice(0, cut), slice(cut, block_rows))
-    halves = [grp_swap(across_part[span], 1) for span in spans]
-    mine, near_part, across = pl.pallas_call(
+    )(*left, met)
+    halves = [grp_swap(part, 1) for part in across_parts]
+    mine, near_part = pl.pallas_call(
         lambda *refs: rest_kernel(grad_scale, *refs),
         grid=(block_rows // TILE,),
-        in_specs=[scalar, tiled(columns), whole],
-        out_specs=[tiled(feat_width)] * 3,
-        out_shape=[
-            shaped(feat_width, jnp.float32),
-            shaped(feat_width, jnp.bfloat16),
-            shaped(feat_width, jnp.float32),
-        ],
+        in_specs=[tiled(columns), whole],
+        out_specs=[tiled(feat_width)] * 2,
+        out_shape=[shaped(feat_width, jnp.float32), shaped(feat_width, jnp.bfloat16)],
         compiler_params=params,
-    )(first, weight, met)
+    )(weight, met)
     crossed = []
-    for span, got in zip(spans, halves):
-        total = across[span] + got.astype(jnp.float32)
-        crossed.append(grp_swap(total.astype(jnp.bfloat16), 2))
-    near_part = grp_swap(near_part, 1).astype(jnp.float32)
-    across = jnp.concatenate(crossed).astype(jnp.float32)
-    grads = mine + near_part + across
+    for step, got in enumerate(halves):
+        total = pl.pallas_call(
+            lambda *refs: total_kernel(grad_scale, 2, *refs),
+            grid=(1,),
+            in_specs=[
+                pl.BlockSpec((TILE, columns), lambda i, step=step: (step, 0)),
+                whole,
+                once,
+            ],
+            out_specs=once,
+            out_shape=jax.ShapeDtypeStruct((TILE, feat_width), jnp.bfloat16),
+            compiler_params=params,
+        )(weight, met, got)
+        crossed.append(grp_swap(total, 2))
+    near_part, proof, _ = lax.optimization_barrier((near_part, proof, total))
+    grads = pl.pallas_call(
+        final_kernel,
+        grid=(block_rows // TILE,),
+        in_specs=[tiled(feat_width)] * 2 + [once] * len(crossed),
+        out_specs=tiled(feat_width),
+        out_shape=shaped(feat_width, jnp.float32),
+        compiler_params=params,
+    )(mine, grp_swap(near_part, 1), *crossed)
     proofs = jnp.broadcast_to(proof.reshape(1, block_rows), (groups, block_rows))
     proof = jnp.sum(lax.all_to_all(proofs, "grp", 0, 0), axis=0)
     return (proof, grads)

time: 191 us -> 206 us (1.079)
  blocking collectives: 57.2 us -> 19.9 us
  waiting for transfers between devices: 96.1 us -> 124 us
  starting transfers between devices: 15.2 us -> 33.9 us
  Pallas kernels: 7.61 us -> 10.2 us
    all_to_all x1 -> x0, blocking collectives: 37.3 us -> none  [on_device(): own_rows = lax.all_to_all(both, 'grp', 0, 0)]
    ppermute x1 -> x2, waiting for transfers between devices: 14.3 us -> 34.4 us  [far_swap(): return lax.ppermute(value, ('blk', 'grp'), pairs)]
    ppermute x8 -> x11, starting transfers between devices: 7.69 us -> 20.2 us  [grp_swap(): return lax.ppermute(value, 'grp', [(k, k ^ distance) for k in range(size)])]
    ppermute x8 -> x11, waiting for transfers between devices: 21.1 us -> 32.3 us  [grp_swap(): return lax.ppermute(value, 'grp', [(k, k ^ distance) for k in range(size)])]
    ppermute x1 -> x2, starting transfers between devices: 3.05 us -> 9.62 us  [far_swap(): return lax.ppermute(value, ('blk', 'grp'), pairs)]
    ppermute x2, waiting for transfers between devices: 60.8 us -> 57.4 us  [blk_swap(): return lax.ppermute(value, 'blk', [(b, b ^ mask) for b in range(blocks)])]
    pallas_call x0 -> x3, Pallas kernels: none -> 2.76 us  [the longest x2 1.59 us: on_device(): pl.pallas_call(lambda *refs: total_kernel(grad_scale, 2, *refs), grid=(1,...]
    add x1 -> x0, other arithmetic: 2.39 us -> none  [on_device(): grads = mine + near_part + across]
  transfers between devices with their start and end apart: 11 -> 15, of which waited for: 5 -> 9; matrix products, arithmetic and copies ran while one was open for 4% -> 5% of each run, Pallas kernels for 1% -> 2%
where the time goes in v3:
time: 206 us; the launch traced here: 205 us
  waiting for transfers between devices  124 us (60%)
  starting transfers between devices  33.9 us (16%)
  blocking collectives  19.9 us (10%)
  Pallas kernels  10.2 us (5%)
  local copies, waits for them, and re-layouts  7 us (3%)
  other arithmetic  5.28 us (3%)
  between operations  4.69 us (2%)
    ppermute x2, waiting for transfers between devices, blk_swap(): return lax.ppermute(value, 'blk', [(b, b ^ mask) for b in range(blocks)])  57.4 us
    ppermute x2, waiting for transfers between devices, far_swap(): return lax.ppermute(value, ('blk', 'grp'), pairs)  34.4 us
    ppermute x11, waiting for transfers between devices, grp_swap(): return lax.ppermute(value, 'grp', [(k, k ^ distance) for k in range(size)])  32.3 us
    ppermute x11, starting transfers between devices, grp_swap(): return lax.ppermute(value, 'grp', [(k, k ^ distance) for k in range(size)])  20.2 us
    all_to_all x1, blocking collectives, on_device(): proof = jnp.sum(lax.all_to_all(proofs, 'grp', 0, 0), axis=0)  19.9 us
    ppermute x2, starting transfers between devices, far_swap(): return lax.ppermute(value, ('blk', 'grp'), pairs)  9.62 us
    pallas_call x1, Pallas kernels, on_device(): pl.pallas_call(lambda *refs: weight_kernel(full_width, grad_scale, wit_sc...  5.35 us
    dynamic_update_slice x2, local copies, waits for them, and re-layouts, put(): return lax.dynamic_update_slice(met, got, (0, index * 2 * share, 0))  4.93 us
  transfers between devices with their start and end apart: 15, of which 9 were waited for; matrix products, arithmetic and copies ran while one was open for 5% of the time, Pallas kernels for 2%

profile of v3, /device:TPU:6, one launch (start us, length us, event | category | flops | bytes accessed | tf_op | source)
XLA Modules:
  0.0 205.0 jit_solution(12525269542120216370)
XLA Ops:
  4.3 3.4 %collective-permute-start.33 = (bf16[320,512]{1,0:T(8,128)(2,1)S(1)}, bf16[320,512]{1,0:T(8,128)(2,1)S(1)}, u32[]{:S(2)}, u32[]{:S(2)}) collective-permute-start(bf16[320,512]{1,0:T(8,128)(2,1)S(1)} %pad_maximum_fusion.5), channel_id=1, source_target_pairs={{0,2},{1,3},{2,0},{3,1},{4,6},{5,7},{6,4},{7,5},{8,10},{9,11},{10,... | collective-permute-start | bytes 983048 | tf_op jit(solution)/shard_map/ppermute | solution.py:14
  12.2 6.0 %collective-permute-done.32 = bf16[320,512]{1,0:T(8,128)(2,1)S(1)} collective-permute-done((bf16[320,512]{1,0:T(8,128)(2,1)S(1)}, bf16[320,512]{1,0:T(8,128)(2,1)S(1)}, u32[]{:S(2)}, u32[]{:S(2)}) %collective-permute-start.32) | collective-permute-done | bytes 327712 | tf_op jit(solution)/shard_map/ppermute | solution.py:14
  19.1 5.3 %collective-permute-start.39 = (bf16[2,320,512]{2,1,0:T(8,128)(2,1)}, bf16[2,320,512]{2,1,0:T(8,128)(2,1)}, u32[]{:S(2)}, u32[]{:S(2)}) collective-permute-start(bf16[2,320,512]{2,1,0:T(8,128)(2,1)} %pad_maximum_fusion.3), channel_id=1, source_target_pairs={{0,11},{1,10},{2,9},{3,8},{4,15},{5,14},{6,13},{7,12},{8,3},{9,2},... | collective-permute-start | bytes 1966088 | tf_op jit(solution)/shard_map/ppermute | solution.py:29
  24.4 2.8 %collective-permute-done.33 = bf16[320,512]{1,0:T(8,128)(2,1)S(1)} collective-permute-done((bf16[320,512]{1,0:T(8,128)(2,1)S(1)}, bf16[320,512]{1,0:T(8,128)(2,1)S(1)}, u32[]{:S(2)}, u32[]{:S(2)}) %collective-permute-start.33) | collective-permute-done | bytes 327712 | tf_op jit(solution)/shard_map/ppermute | solution.py:14
  27.3 3.3 %collective-permute-done.34 = bf16[320,512]{1,0:T(8,128)(2,1)S(1)} collective-permute-done((bf16[320,512]{1,0:T(8,128)(2,1)S(1)}, bf16[320,512]{1,0:T(8,128)(2,1)S(1)}, u32[]{:S(2)}, u32[]{:S(2)}) %collective-permute-start.34) | collective-permute-done | bytes 327712 | tf_op jit(solution)/shard_map/ppermute | solution.py:14
  31.5 4.3 %collective-permute-start.38 = (bf16[2,320,512]{2,1,0:T(8,128)(2,1)}, bf16[2,320,512]{2,1,0:T(8,128)(2,1)}, u32[]{:S(2)}, u32[]{:S(2)}) collective-permute-start(bf16[2,320,512]{2,1,0:T(8,128)(2,1)} %pad_maximum_fusion.2), channel_id=1, source_target_pairs={{0,11},{1,10},{2,9},{3,8},{4,15},{5,14},{6,13},{7,12},{8,3},{9,2},... | collective-permute-start | bytes 1966088 | tf_op jit(solution)/shard_map/ppermute | solution.py:29
  36.0 7.1 %collective-permute-start.35 = (bf16[640,512]{1,0:T(8,128)(2,1)S(1)}, bf16[640,512]{1,0:T(8,128)(2,1)S(1)}, u32[]{:S(2)}, u32[]{:S(2)}) collective-permute-start(bf16[640,512]{1,0:T(8,128)(2,1)S(1)} %copy-done), channel_id=1, source_target_pairs={{0,1},{1,0},{2,3},{3,2},{4,5},{5,4},{6,7},{7,6},{8,9},{9,8},{10,11... | collective-permute-start | bytes 1966088 | tf_op jit(solution)/shard_map/ppermute | solution.py:14
  45.6 9.1 %collective-permute-done.39 = bf16[2,320,512]{2,1,0:T(8,128)(2,1)} collective-permute-done((bf16[2,320,512]{2,1,0:T(8,128)(2,1)}, bf16[2,320,512]{2,1,0:T(8,128)(2,1)}, u32[]{:S(2)}, u32[]{:S(2)}) %collective-permute-start.39) | collective-permute-done | bytes 655392 | tf_op jit(solution)/shard_map/ppermute | solution.py:29
  54.7 25.3 %collective-permute-done.38 = bf16[2,320,512]{2,1,0:T(8,128)(2,1)} collective-permute-done((bf16[2,320,512]{2,1,0:T(8,128)(2,1)}, bf16[2,320,512]{2,1,0:T(8,128)(2,1)}, u32[]{:S(2)}, u32[]{:S(2)}) %collective-permute-start.38) | collective-permute-done | bytes 655392 | tf_op jit(solution)/shard_map/ppermute | solution.py:29
  82.4 66.5 %while.25 = (s32[]{:T(128)}, bf16[4,640,512]{2,1,0:T(8,128)(2,1)}, s32[]{:T(128)}, bf16[4,320,512]{2,1,0:T(8,128)(2,1)}, s32[]{:T(128)}, /*index=5*/s32[]{:T(128)}, s32[]{:T(128)}, s32[]{:T(128)}, s32[]{:T(128)}) while((s32[]{:T(128)}, bf16[4,640,512]{2,1,0:T(8,128)(2,1)}, s32[]{:T(128)}, bf16[4,320,512]{2,1,0:T(8,128)(2,1)}, s32[]{:T(128)}, ...), condition=%wide.region_39.40_spmd, body=%wide.region_20.39_spmd.sunk | while | flops 11 | bytes 13107549 | solution.py:157
  82.4 30.2 %conditional.10 = (bf16[4,320,512]{2,1,0:T(8,128)(2,1)}) conditional(s32[]{:T(128)} %clamp.9, bf16[4,320,512]{2,1,0:T(8,128)(2,1)} %get-tuple-element.368, bf16[4,320,512]{2,1,0:T(8,128)(2,1)} %get-tuple-element.368, bf16[4,320,512]{2,1,0:T(8,128)(2,1)} %get-tuple-element.368, ...), branch_computations={%region_21.21_spmd, %region_22.22_spmd, %region_23.23_spmd, %regio... | conditional | bytes 5242928 | solution.py:36
  83.3 29.3 %collective-permute-done.18 = bf16[4,320,512]{2,1,0:T(8,128)(2,1)} collective-permute-done((bf16[4,320,512]{2,1,0:T(8,128)(2,1)}, bf16[4,320,512]{2,1,0:T(8,128)(2,1)}, u32[]{:S(2)}, u32[]{:S(2)}) %collective-permute-start.18) | collective-permute-done | bytes 1310752 | tf_op jit(solution)/shard_map/while/body/cond/branch_4_fun/ppermute | solution.py:19
  112.6 2.5 %conditional.11 = (bf16[4,640,512]{2,1,0:T(8,128)(2,1)}) conditional(s32[]{:T(128)} %convert_element_type.9, (s32[]{:T(128)}, bf16[4,640,512]{2,1,0:T(8,128)(2,1)}, bf16[4,320,512]{2,1,0:T(8,128)(2,1)}) %tuple.166, (bf16[4,320,512]{2,1,0:T(8,128)(2,1)}, s32[]{:T(128)}, bf16[4,640,512]{2,1,0:T(8,128)(2,1)}) %tuple.167), branch_computations={%region_37.37_spmd, %region_38.38_spmd} | conditional | flops 4 | bytes 7864418 | solution.py:141
  112.6 2.5 %constant_dynamic-update-slice_fusion.2 = bf16[4,640,512]{2,1,0:T(8,128)(2,1)} fusion(bf16[4,640,512]{2,1,0:T(8,128)(2,1)} %get-tuple-element.154, bf16[4,320,512]{2,1,0:T(8,128)(2,1)} %get-tuple-element.155, s32[]{:T(128)S(6)} %select_n.27), kind=kLoop, calls=%fused_computation.2 | loop fusion | bytes 2621444 | tf_op jit(solution)/shard_map/while/body/cond/branch_0_fun/dynamic_update_slice | solution.py:135
  115.1 31.4 %conditional.10 = (bf16[4,320,512]{2,1,0:T(8,128)(2,1)}) conditional(s32[]{:T(128)} %clamp.9, bf16[4,320,512]{2,1,0:T(8,128)(2,1)} %get-tuple-element.368, bf16[4,320,512]{2,1,0:T(8,128)(2,1)} %get-tuple-element.368, bf16[4,320,512]{2,1,0:T(8,128)(2,1)} %get-tuple-element.368, ...), branch_computations={%region_21.21_spmd, %region_22.22_spmd, %region_23.23_spmd, %regio... | conditional | bytes 5242928 | solution.py:36
  115.1 3.3 %collective-permute-start.21 = (bf16[4,320,512]{2,1,0:T(8,128)(2,1)}, bf16[4,320,512]{2,1,0:T(8,128)(2,1)}, u32[]{:S(2)}, u32[]{:S(2)}) collective-permute-start(bf16[4,320,512]{2,1,0:T(8,128)(2,1)} %param.27), channel_id=1, source_target_pairs={{0,112},{4,116},{8,120},{12,124},{16,96},{20,100},{24,104},{28,108... | collective-permute-start | bytes 3932168 | tf_op jit(solution)/shard_map/while/body/cond/branch_7_fun/ppermute | solution.py:19
  118.4 28.1 %collective-permute-done.21 = bf16[4,320,512]{2,1,0:T(8,128)(2,1)} collective-permute-done((bf16[4,320,512]{2,1,0:T(8,128)(2,1)}, bf16[4,320,512]{2,1,0:T(8,128)(2,1)}, u32[]{:S(2)}, u32[]{:S(2)}) %collective-permute-start.21) | collective-permute-done | bytes 1310752 | tf_op jit(solution)/shard_map/while/body/cond/branch_7_fun/ppermute | solution.py:19
  146.5 2.5 %conditional.11 = (bf16[4,640,512]{2,1,0:T(8,128)(2,1)}) conditional(s32[]{:T(128)} %convert_element_type.9, (s32[]{:T(128)}, bf16[4,640,512]{2,1,0:T(8,128)(2,1)}, bf16[4,320,512]{2,1,0:T(8,128)(2,1)}) %tuple.166, (bf16[4,320,512]{2,1,0:T(8,128)(2,1)}, s32[]{:T(128)}, bf16[4,640,512]{2,1,0:T(8,128)(2,1)}) %tuple.167), branch_computations={%region_37.37_spmd, %region_38.38_spmd} | conditional | flops 4 | bytes 7864418 | solution.py:141
  146.5 2.5 %constant_dynamic-update-slice_fusion.2 = bf16[4,640,512]{2,1,0:T(8,128)(2,1)} fusion(bf16[4,640,512]{2,1,0:T(8,128)(2,1)} %get-tuple-element.154, bf16[4,320,512]{2,1,0:T(8,128)(2,1)} %get-tuple-element.155, s32[]{:T(128)S(6)} %select_n.27), kind=kLoop, calls=%fused_computation.2 | loop fusion | bytes 2621444 | tf_op jit(solution)/shard_map/while/body/cond/branch_0_fun/dynamic_update_slice | solution.py:135
  148.9 5.3 %shard_map.51 = (f32[640,1]{1,0:T(8,128)S(1)}, bf16[640,640]{1,0:T(8,128)(2,1)S(1)}, bf16[320,512]{1,0:T(8,128)(2,1)S(1)}, bf16[320,512]{1,0:T(8,128)(2,1)S(1)}) custom-call(bf16[640,512]{1,0:T(8,128)(2,1)S(1)} %copy-done, bf16[640,512]{1,0:T(8,128)(2,1)S(1)} %collective-permute-done.35.refs_1_, bf16[640,512]{1,0:T(8,128)(2,1)S(1)} %collective-permute-done.36.refs_2_, ...), custom_call_target="tpu_custom_call" | custom-call | tf_op jit(solution)/shard_map/pallas_call | solution.py:169
  158.5 6.5 %collective-permute-done.40.refs_2_ = bf16[320,512]{1,0:T(8,128)(2,1)S(1)} collective-permute-done((bf16[320,512]{1,0:T(8,128)(2,1)S(1)}, bf16[320,512]{1,0:T(8,128)(2,1)S(1)}, u32[]{:S(2)}, u32[]{:S(2)}) %collective-permute-start.40) | collective-permute-done | bytes 327712 | tf_op jit(solution)/shard_map/ppermute | solution.py:14
  165.6 13.5 %collective-permute-done.42.refs_2_ = bf16[320,512]{1,0:T(8,128)(2,1)S(1)} collective-permute-done((bf16[320,512]{1,0:T(8,128)(2,1)S(1)}, bf16[320,512]{1,0:T(8,128)(2,1)S(1)}, u32[]{:S(2)}, u32[]{:S(2)}) %collective-permute-start.42) | collective-permute-done | bytes 327712 | tf_op jit(solution)/shard_map/ppermute | solution.py:14
  180.3 2.9 %collective-permute-start.44 = (bf16[320,512]{1,0:T(8,128)(2,1)S(1)}, bf16[320,512]{1,0:T(8,128)(2,1)S(1)}, u32[]{:S(2)}, u32[]{:S(2)}) collective-permute-start(bf16[320,512]{1,0:T(8,128)(2,1)S(1)} %shard_map.53), channel_id=1, source_target_pairs={{0,2},{1,3},{2,0},{3,1},{4,6},{5,7},{6,4},{7,5},{8,10},{9,11},{10,... | collective-permute-start | bytes 983048 | tf_op jit(solution)/shard_map/ppermute | solution.py:14
  183.4 19.9 %all_to_all.6 = f32[4,1,640]{2,1,0:T(1,128)S(1)} all-to-all(f32[4,1,640]{2,1,0:T(1,128)S(1)} %broadcast_in_dim.8), channel_id=1, replica_groups=mesh['blk'=64,'grp'=4] {'grp'}, dimensions={0} | all-to-all | bytes 20480 | tf_op jit(solution)/shard_map/all_to_all | solution.py:212
  (40 shorter events, 19.8 us)
Async XLA Ops:
  2.2 5.6 %copy-start.2 = (s32[2,64]{1,0:T(2,128)S(1)}, s32[2,64]{1,0:T(2,128)}, u32[]{:S(2)}) copy-start(s32[2,64]{1,0:T(2,128)} %param.45) | copy-start | bytes 1540
  2.2 16.0 %collective-permute-start.32 = (bf16[320,512]{1,0:T(8,128)(2,1)S(1)}, bf16[320,512]{1,0:T(8,128)(2,1)S(1)}, u32[]{:S(2)}, u32[]{:S(2)}) collective-permute-start(bf16[320,512]{1,0:T(8,128)(2,1)S(1)} %pad_maximum_fusion.4), channel_id=1, source_target_pairs={{0,1},{1,0},{2,3},{3,2},{4,5},{5,4},{6,7},{7,6},{8,9},{9,8},{10,11... | collective-permute-start | bytes 983048 | tf_op jit(solution)/shard_map/ppermute | solution.py:14
  4.3 23.0 %collective-permute-start.33 = (bf16[320,512]{1,0:T(8,128)(2,1)S(1)}, bf16[320,512]{1,0:T(8,128)(2,1)S(1)}, u32[]{:S(2)}, u32[]{:S(2)}) collective-permute-start(bf16[320,512]{1,0:T(8,128)(2,1)S(1)} %pad_maximum_fusion.5), channel_id=1, source_target_pairs={{0,2},{1,3},{2,0},{3,1},{4,6},{5,7},{6,4},{7,5},{8,10},{9,11},{10,... | collective-permute-start | bytes 983048 | tf_op jit(solution)/shard_map/ppermute | solution.py:14
  7.6 23.0 %collective-permute-start.34 = (bf16[320,512]{1,0:T(8,128)(2,1)S(1)}, bf16[320,512]{1,0:T(8,128)(2,1)S(1)}, u32[]{:S(2)}, u32[]{:S(2)}) collective-permute-start(bf16[320,512]{1,0:T(8,128)(2,1)S(1)} %pad_maximum_fusion.6), channel_id=1, source_target_pairs={{0,3},{1,2},{2,1},{3,0},{4,7},{5,6},{6,5},{7,4},{8,11},{9,10},{10,... | collective-permute-start | bytes 983048 | tf_op jit(solution)/shard_map/ppermute | solution.py:14
  19.1 35.6 %collective-permute-start.39 = (bf16[2,320,512]{2,1,0:T(8,128)(2,1)}, bf16[2,320,512]{2,1,0:T(8,128)(2,1)}, u32[]{:S(2)}, u32[]{:S(2)}) collective-permute-start(bf16[2,320,512]{2,1,0:T(8,128)(2,1)} %pad_maximum_fusion.3), channel_id=1, source_target_pairs={{0,11},{1,10},{2,9},{3,8},{4,15},{5,14},{6,13},{7,12},{8,3},{9,2},... | collective-permute-start | bytes 1966088 | tf_op jit(solution)/shard_map/ppermute | solution.py:29
  31.5 4.5 %copy-start = (bf16[640,512]{1,0:T(8,128)(2,1)S(1)}, bf16[640,512]{1,0:T(8,128)(2,1)}, u32[]{:S(2)}) copy-start(bf16[640,512]{1,0:T(8,128)(2,1)} %refs_0_) | copy-start | bytes 1966084
  31.5 48.5 %collective-permute-start.38 = (bf16[2,320,512]{2,1,0:T(8,128)(2,1)}, bf16[2,320,512]{2,1,0:T(8,128)(2,1)}, u32[]{:S(2)}, u32[]{:S(2)}) collective-permute-start(bf16[2,320,512]{2,1,0:T(8,128)(2,1)} %pad_maximum_fusion.2), channel_id=1, source_target_pairs={{0,11},{1,10},{2,9},{3,8},{4,15},{5,14},{6,13},{7,12},{8,3},{9,2},... | collective-permute-start | bytes 1966088 | tf_op jit(solution)/shard_map/ppermute | solution.py:29
  36.0 112.9 %collective-permute-start.35 = (bf16[640,512]{1,0:T(8,128)(2,1)S(1)}, bf16[640,512]{1,0:T(8,128)(2,1)S(1)}, u32[]{:S(2)}, u32[]{:S(2)}) collective-permute-start(bf16[640,512]{1,0:T(8,128)(2,1)S(1)} %copy-done), channel_id=1, source_target_pairs={{0,1},{1,0},{2,3},{3,2},{4,5},{5,4},{6,7},{7,6},{8,9},{9,8},{10,11... | collective-permute-start | bytes 1966088 | tf_op jit(solution)/shard_map/ppermute | solution.py:14
  43.1 105.8 %collective-permute-start.36 = (bf16[640,512]{1,0:T(8,128)(2,1)S(1)}, bf16[640,512]{1,0:T(8,128)(2,1)S(1)}, u32[]{:S(2)}, u32[]{:S(2)}) collective-permute-start(bf16[640,512]{1,0:T(8,128)(2,1)S(1)} %copy-done), channel_id=1, source_target_pairs={{0,2},{1,3},{2,0},{3,1},{4,6},{5,7},{6,4},{7,5},{8,10},{9,11},{10,... | collective-permute-start | bytes 1966088 | tf_op jit(solution)/shard_map/ppermute | solution.py:14
  43.7 105.2 %collective-permute-start.37 = (bf16[640,512]{1,0:T(8,128)(2,1)S(1)}, bf16[640,512]{1,0:T(8,128)(2,1)S(1)}, u32[]{:S(2)}, u32[]{:S(2)}) collective-permute-start(bf16[640,512]{1,0:T(8,128)(2,1)S(1)} %copy-done), channel_id=1, source_target_pairs={{0,3},{1,2},{2,1},{3,0},{4,7},{5,6},{6,5},{7,4},{8,11},{9,10},{10,... | collective-permute-start | bytes 1966088 | tf_op jit(solution)/shard_map/ppermute | solution.py:14
  82.4 30.2 %collective-permute-start.18 = (bf16[4,320,512]{2,1,0:T(8,128)(2,1)}, bf16[4,320,512]{2,1,0:T(8,128)(2,1)}, u32[]{:S(2)}, u32[]{:S(2)}) collective-permute-start(bf16[4,320,512]{2,1,0:T(8,128)(2,1)} %param.24), channel_id=1, source_target_pairs={{0,64},{4,68},{8,72},{12,76},{16,80},{20,84},{24,88},{28,92},{32,9... | collective-permute-start | bytes 3932168 | tf_op jit(solution)/shard_map/while/body/cond/branch_4_fun/ppermute | solution.py:19
  115.1 31.4 %collective-permute-start.21 = (bf16[4,320,512]{2,1,0:T(8,128)(2,1)}, bf16[4,320,512]{2,1,0:T(8,128)(2,1)}, u32[]{:S(2)}, u32[]{:S(2)}) collective-permute-start(bf16[4,320,512]{2,1,0:T(8,128)(2,1)} %param.27), channel_id=1, source_target_pairs={{0,112},{4,116},{8,120},{12,124},{16,96},{20,100},{24,104},{28,108... | collective-permute-start | bytes 3932168 | tf_op jit(solution)/shard_map/while/body/cond/branch_7_fun/ppermute | solution.py:19
  148.9 7.5 %copy-start.1 = (bf16[4,640,512]{2,1,0:T(8,128)(2,1)S(1)}, bf16[4,640,512]{2,1,0:T(8,128)(2,1)}, u32[]{:S(2)}) copy-start(bf16[4,640,512]{2,1,0:T(8,128)(2,1)} %get-tuple-element.203.refs_4_.refs_1_) | copy-start | bytes 7864324
  154.3 10.7 %collective-permute-start.40 = (bf16[320,512]{1,0:T(8,128)(2,1)S(1)}, bf16[320,512]{1,0:T(8,128)(2,1)S(1)}, u32[]{:S(2)}, u32[]{:S(2)}) collective-permute-start(bf16[320,512]{1,0:T(8,128)(2,1)S(1)} %get-tuple-element.207), channel_id=1, source_target_pairs={{0,1},{1,0},{2,3},{3,2},{4,5},{5,4},{6,7},{7,6},{8,9},{9,8},{10,11... | collective-permute-start | bytes 983048 | tf_op jit(solution)/shard_map/ppermute | solution.py:14
  154.4 24.7 %collective-permute-start.42 = (bf16[320,512]{1,0:T(8,128)(2,1)S(1)}, bf16[320,512]{1,0:T(8,128)(2,1)S(1)}, u32[]{:S(2)}, u32[]{:S(2)}) collective-permute-start(bf16[320,512]{1,0:T(8,128)(2,1)S(1)} %get-tuple-element.211), channel_id=1, source_target_pairs={{0,1},{1,0},{2,3},{3,2},{4,5},{5,4},{6,7},{7,6},{8,9},{9,8},{10,11... | collective-permute-start | bytes 983048 | tf_op jit(solution)/shard_map/ppermute | solution.py:14
  165.5 38.4 %collective-permute-start.41 = (bf16[640,512]{1,0:T(8,128)(2,1)}, bf16[640,512]{1,0:T(8,128)(2,1)S(1)}, u32[]{:S(2)}, u32[]{:S(2)}) collective-permute-start(bf16[640,512]{1,0:T(8,128)(2,1)} %get-tuple-element.210), channel_id=1, source_target_pairs={{0,1},{1,0},{2,3},{3,2},{4,5},{5,4},{6,7},{7,6},{8,9},{9,8},{10,11... | collective-permute-start | bytes 1966088 | tf_op jit(solution)/shard_map/ppermute | solution.py:14
  180.3 23.6 %collective-permute-start.43 = (bf16[320,512]{1,0:T(8,128)(2,1)}, bf16[320,512]{1,0:T(8,128)(2,1)S(1)}, u32[]{:S(2)}, u32[]{:S(2)}) collective-permute-start(bf16[320,512]{1,0:T(8,128)(2,1)} %shard_map.54), channel_id=1, source_target_pairs={{0,2},{1,3},{2,0},{3,1},{4,6},{5,7},{6,4},{7,5},{8,10},{9,11},{10,... | collective-permute-start | bytes 983048 | tf_op jit(solution)/shard_map/ppermute | solution.py:14
  180.3 23.6 %collective-permute-start.44 = (bf16[320,512]{1,0:T(8,128)(2,1)S(1)}, bf16[320,512]{1,0:T(8,128)(2,1)S(1)}, u32[]{:S(2)}, u32[]{:S(2)}) collective-permute-start(bf16[320,512]{1,0:T(8,128)(2,1)S(1)} %shard_map.53), channel_id=1, source_target_pairs={{0,2},{1,3},{2,0},{3,1},{4,6},{5,7},{6,4},{7,5},{8,10},{9,11},{10,... | collective-permute-start | bytes 983048 | tf_op jit(solution)/shard_map/ppermute | solution.py:14

commit v4 on v3

--- a/solution.py
+++ b/solution.py
@@ -114,9 +114,6 @@
     pieces = [chunk_for(here)]
     for distance in range(1, groups):
         pieces.append(grp_swap(chunk_for(here ^ distance), distance))
-    late = far_swap(jnp.stack(pieces[:1:-1]))
-    early = far_swap(jnp.stack(pieces[1::-1]))
-    own_rows = jnp.stack(pieces)
     masks = [partners[r, 0] for r in range(rounds_count)]
     far_bits = [(m >> 1) & 1 for m in masks]
     swapped = far_bits[0] > far_bits[1]
@@ -126,10 +123,14 @@
     ]
     near_count = rounds_count - far_bits[0] - far_bits[1]
     met = untouched((groups, rounds_count * 2 * share, feat_width), generated.dtype)
-    own_rows, generated, masks, near_count, met = lax.optimization_barrier(
-        (own_rows, generated, masks, near_count, met)
+    pieces[1], masks, near_count, met = lax.optimization_barrier(
+        (pieces[1], masks, near_count, met)
     )
-    left = [generated] + [grp_swap(generated, d) for d in range(1, groups)]
+    late = far_swap(jnp.stack(pieces[:1:-1]))
+    early = far_swap(jnp.stack(pieces[1::-1]))
+    own_rows = jnp.stack(pieces)
+    own_rows, generated = lax.optimization_barrier((own_rows, generated))
+    others = [grp_swap(generated, d) for d in range(2, groups)]
 
     def put(met, got, index):
         return lax.dynamic_update_slice(met, got, (0, index * 2 * share, 0))
@@ -152,7 +153,10 @@
 
     carry = (met, *masks)
     carry = lax.fori_loop(0, near_count, meet(own_rows), carry)
-    carry, late, early = lax.optimization_barrier((carry, late, early))
+    carry, late, early, generated = lax.optimization_barrier(
+        (carry, late, early, generated)
+    )
+    left = [generated, grp_swap(generated, 1)] + others
     far_rows = jnp.concatenate([late, early])
     met, _, _ = lax.fori_loop(near_count, rounds_count, meet(far_rows), carry)
 

time: 206 us -> 176 us (0.85)
  waiting for transfers between devices: 124 us -> 85.5 us
  blocking collectives: 19.9 us -> 25.6 us
  starting transfers between devices: 33.9 us -> 36 us
    ppermute x2, waiting for transfers between devices: 34.4 us -> 0.01 us  [far_swap(): return lax.ppermute(value, ('blk', 'grp'), pairs)]
    ppermute x11, waiting for transfers between devices: 32.3 us -> 23.5 us  [grp_swap(): return lax.ppermute(value, 'grp', [(k, k ^ distance) for k in range(size)])]
    all_to_all x1, blocking collectives: 19.9 us -> 25.6 us  [on_device(): proof = jnp.sum(lax.all_to_all(proofs, 'grp', 0, 0), axis=0)]
    ppermute x2 -> x3, waiting for transfers between devices: 57.4 us -> 62.1 us  [blk_swap(): return lax.ppermute(value, 'blk', [(b, b ^ mask) for b in range(blocks)])]
    ppermute x2 -> x3, starting transfers between devices: 4.11 us -> 4.51 us  [blk_swap(): return lax.ppermute(value, 'blk', [(b, b ^ mask) for b in range(blocks)])]
  transfers between devices with their start and end apart: 15 -> 16, of which waited for: 9 -> 8; matrix products, arithmetic and copies ran while one was open for 5% -> 6% of each run, Pallas kernels for 2% -> 2%
where the time goes in v4:
time: 176 us; the launch traced here: 175 us
  waiting for transfers between devices  85.5 us (49%)
  starting transfers between devices  36 us (20%)
  blocking collectives  25.6 us (15%)
  Pallas kernels  10.2 us (6%)
  local copies, waits for them, and re-layouts  7.92 us (4%)
  other arithmetic  5.28 us (3%)
  between operations  4.67 us (3%)
    ppermute x3, waiting for transfers between devices, blk_swap(): return lax.ppermute(value, 'blk', [(b, b ^ mask) for b in range(blocks)])  62.1 us
    all_to_all x1, blocking collectives, on_device(): proof = jnp.sum(lax.all_to_all(proofs, 'grp', 0, 0), axis=0)  25.6 us
    ppermute x11, waiting for transfers between devices, grp_swap(): return lax.ppermute(value, 'grp', [(k, k ^ distance) for k in range(size)])  23.5 us
    ppermute x11, starting transfers between devices, grp_swap(): return lax.ppermute(value, 'grp', [(k, k ^ distance) for k in range(size)])  21.9 us
    ppermute x2, starting transfers between devices, far_swap(): return lax.ppermute(value, ('blk', 'grp'), pairs)  9.62 us
    pallas_call x1, Pallas kernels, on_device(): pl.pallas_call(lambda *refs: weight_kernel(full_width, grad_scale, wit_sc...  5.34 us
    dynamic_update_slice x2, local copies, waits for them, and re-layouts, put(): return lax.dynamic_update_slice(met, got, (0, index * 2 * share, 0))  4.93 us
    ppermute x3, starting transfers between devices, blk_swap(): return lax.ppermute(value, 'blk', [(b, b ^ mask) for b in range(blocks)])  4.51 us
  transfers between devices with their start and end apart: 16, of which 8 were waited for; matrix products, arithmetic and copies ran while one was open for 6% of the time, Pallas kernels for 2%

profile of v4, /device:TPU:6, one launch (start us, length us, event | category | flops | bytes accessed | tf_op | source)
XLA Modules:
  0.0 175.2 jit_solution(4416592966571031150)
XLA Ops:
  4.3 3.4 %collective-permute-start.33 = (bf16[320,512]{1,0:T(8,128)(2,1)S(1)}, bf16[320,512]{1,0:T(8,128)(2,1)S(1)}, u32[]{:S(2)}, u32[]{:S(2)}) collective-permute-start(bf16[320,512]{1,0:T(8,128)(2,1)S(1)} %pad_maximum_fusion.5), channel_id=1, source_target_pairs={{0,2},{1,3},{2,0},{3,1},{4,6},{5,7},{6,4},{7,5},{8,10},{9,11},{10,... | collective-permute-start | bytes 983048 | tf_op jit(solution)/shard_map/ppermute | solution.py:14
  12.2 6.0 %collective-permute-done.32 = bf16[320,512]{1,0:T(8,128)(2,1)S(1)} collective-permute-done((bf16[320,512]{1,0:T(8,128)(2,1)S(1)}, bf16[320,512]{1,0:T(8,128)(2,1)S(1)}, u32[]{:S(2)}, u32[]{:S(2)}) %collective-permute-start.32) | collective-permute-done | bytes 327712 | tf_op jit(solution)/shard_map/ppermute | solution.py:14
  19.1 5.3 %collective-permute-start.36 = (bf16[2,320,512]{2,1,0:T(8,128)(2,1)}, bf16[2,320,512]{2,1,0:T(8,128)(2,1)}, u32[]{:S(2)}, u32[]{:S(2)}) collective-permute-start(bf16[2,320,512]{2,1,0:T(8,128)(2,1)} %pad_maximum_fusion.3), channel_id=1, source_target_pairs={{0,11},{1,10},{2,9},{3,8},{4,15},{5,14},{6,13},{7,12},{8,3},{9,2},... | collective-permute-start | bytes 1966088 | tf_op jit(solution)/shard_map/ppermute | solution.py:29
  24.4 2.8 %collective-permute-done.33 = bf16[320,512]{1,0:T(8,128)(2,1)S(1)} collective-permute-done((bf16[320,512]{1,0:T(8,128)(2,1)S(1)}, bf16[320,512]{1,0:T(8,128)(2,1)S(1)}, u32[]{:S(2)}, u32[]{:S(2)}) %collective-permute-start.33) | collective-permute-done | bytes 327712 | tf_op jit(solution)/shard_map/ppermute | solution.py:14
  27.3 3.3 %collective-permute-done.34 = bf16[320,512]{1,0:T(8,128)(2,1)S(1)} collective-permute-done((bf16[320,512]{1,0:T(8,128)(2,1)S(1)}, bf16[320,512]{1,0:T(8,128)(2,1)S(1)}, u32[]{:S(2)}, u32[]{:S(2)}) %collective-permute-start.34) | collective-permute-done | bytes 327712 | tf_op jit(solution)/shard_map/ppermute | solution.py:14
  31.5 4.3 %collective-permute-start.35 = (bf16[2,320,512]{2,1,0:T(8,128)(2,1)}, bf16[2,320,512]{2,1,0:T(8,128)(2,1)}, u32[]{:S(2)}, u32[]{:S(2)}) collective-permute-start(bf16[2,320,512]{2,1,0:T(8,128)(2,1)} %pad_maximum_fusion.2), channel_id=1, source_target_pairs={{0,11},{1,10},{2,9},{3,8},{4,15},{5,14},{6,13},{7,12},{8,3},{9,2},... | collective-permute-start | bytes 1966088 | tf_op jit(solution)/shard_map/ppermute | solution.py:29
  36.9 7.5 %collective-permute-start.38 = (bf16[640,512]{1,0:T(8,128)(2,1)S(1)}, bf16[640,512]{1,0:T(8,128)(2,1)S(1)}, u32[]{:S(2)}, u32[]{:S(2)}) collective-permute-start(bf16[640,512]{1,0:T(8,128)(2,1)S(1)} %copy-done), channel_id=1, source_target_pairs={{0,2},{1,3},{2,0},{3,1},{4,6},{5,7},{6,4},{7,5},{8,10},{9,11},{10,... | collective-permute-start | bytes 1966088 | tf_op jit(solution)/shard_map/ppermute | solution.py:14
  46.3 34.6 %while.24 = (s32[]{:T(128)}, bf16[4,640,512]{2,1,0:T(8,128)(2,1)}, s32[]{:T(128)}, s32[]{:T(128)}, bf16[4,320,512]{2,1,0:T(8,128)(2,1)S(1)}, /*index=5*/s32[]{:T(128)}, s32[]{:T(128)}, s32[]{:T(128)}, s32[]{:T(128)}, s32[]{:T(128)}) while((s32[]{:T(128)}, bf16[4,640,512]{2,1,0:T(8,128)(2,1)}, s32[]{:T(128)}, s32[]{:T(128)}, ...), condition=%wide.region_19.20_spmd, body=%wide.region_0.19_spmd.sunk | while | flops 11 | bytes 13107557 | solution.py:155
  46.3 28.7 %conditional.8 = (bf16[4,320,512]{2,1,0:T(8,128)(2,1)}) conditional(s32[]{:T(128)} %clamp.8, bf16[4,320,512]{2,1,0:T(8,128)(2,1)S(1)} %get-tuple-element.345, bf16[4,320,512]{2,1,0:T(8,128)(2,1)S(1)} %get-tuple-element.345, bf16[4,320,512]{2,1,0:T(8,128)(2,1)S(1)} %get-tuple-element.345, ...), branch_computations={%region_1.1_spmd, %region_2.2_spmd, %region_3.3_spmd, %region_4.4_... | conditional | bytes 5242928 | solution.py:36
  47.9 27.2 %collective-permute-done = bf16[4,320,512]{2,1,0:T(8,128)(2,1)} collective-permute-done((bf16[4,320,512]{2,1,0:T(8,128)(2,1)S(1)}, bf16[4,320,512]{2,1,0:T(8,128)(2,1)}, u32[]{:S(2)}, u32[]{:S(2)}) %collective-permute-start) | collective-permute-done | bytes 1310752 | tf_op jit(solution)/shard_map/while/body/cond/branch_1_fun/ppermute | solution.py:19
  75.1 5.8 %conditional.9 = (bf16[4,640,512]{2,1,0:T(8,128)(2,1)}) conditional(s32[]{:T(128)} %convert_element_type.8, (s32[]{:T(128)}, bf16[4,640,512]{2,1,0:T(8,128)(2,1)}, bf16[4,320,512]{2,1,0:T(8,128)(2,1)}) %tuple.165, (bf16[4,320,512]{2,1,0:T(8,128)(2,1)}, s32[]{:T(128)}, bf16[4,640,512]{2,1,0:T(8,128)(2,1)}) %tuple.166), branch_computations={%region_17.17_spmd, %region_18.18_spmd} | conditional | flops 4 | bytes 7864418 | solution.py:142
  75.1 3.4 %collective-permute-done.30 = bf16[4,320,512]{2,1,0:T(8,128)(2,1)} collective-permute-done((bf16[4,320,512]{2,1,0:T(8,128)(2,1)}, bf16[4,320,512]{2,1,0:T(8,128)(2,1)}, u32[]{:S(2)}, u32[]{:S(2)}) %collective-permute-start.30) | collective-permute-done | bytes 1310752 | tf_op jit(solution)/shard_map/while/body/cond/branch_1_fun/ppermute | solution.py:19
  78.4 2.5 %constant_dynamic-update-slice_fusion.1 = bf16[4,640,512]{2,1,0:T(8,128)(2,1)} fusion(bf16[4,640,512]{2,1,0:T(8,128)(2,1)} %get-tuple-element.143, bf16[4,320,512]{2,1,0:T(8,128)(2,1)} %collective-permute-done.30, s32[]{:T(128)S(6)} %select_n.26), kind=kLoop, calls=%fused_computation.1 | loop fusion | bytes 2621444 | tf_op jit(solution)/shard_map/while/body/cond/branch_1_fun/dynamic_update_slice | solution.py:136
  81.0 2.5 %pad_maximum_fusion.1 = bf16[4,320,512]{2,1,0:T(8,128)(2,1)} fusion(bf16[2,320,512]{2,1,0:T(8,128)(2,1)} %collective-permute-done.36, bf16[2,320,512]{2,1,0:T(8,128)(2,1)} %collective-permute-done.35), kind=kLoop, calls=%fused_computation.5 | loop fusion | flops 655360 | bytes 2621440 | tf_op jit(solution)/shard_map/concatenate | solution.py:160
  83.5 36.9 %while.25 = (s32[]{:T(128)}, bf16[4,640,512]{2,1,0:T(8,128)(2,1)}, s32[]{:T(128)}, bf16[4,320,512]{2,1,0:T(8,128)(2,1)}, s32[]{:T(128)}, /*index=5*/s32[]{:T(128)}, s32[]{:T(128)}, s32[]{:T(128)}, s32[]{:T(128)}) while((s32[]{:T(128)}, bf16[4,640,512]{2,1,0:T(8,128)(2,1)}, s32[]{:T(128)}, bf16[4,320,512]{2,1,0:T(8,128)(2,1)}, s32[]{:T(128)}, ...), condition=%wide.region_39.40_spmd, body=%wide.region_20.39_spmd.sunk | while | flops 11 | bytes 13107549 | solution.py:161
  83.5 34.5 %conditional.10 = (bf16[4,320,512]{2,1,0:T(8,128)(2,1)}) conditional(s32[]{:T(128)} %clamp.9, bf16[4,320,512]{2,1,0:T(8,128)(2,1)} %get-tuple-element.372, bf16[4,320,512]{2,1,0:T(8,128)(2,1)} %get-tuple-element.372, bf16[4,320,512]{2,1,0:T(8,128)(2,1)} %get-tuple-element.372, ...), branch_computations={%region_21.21_spmd, %region_22.22_spmd, %region_23.23_spmd, %regio... | conditional | bytes 5242928 | solution.py:36
  83.5 2.9 %collective-permute-start.29 = (bf16[4,320,512]{2,1,0:T(8,128)(2,1)}, bf16[4,320,512]{2,1,0:T(8,128)(2,1)}, u32[]{:S(2)}, u32[]{:S(2)}) collective-permute-start(bf16[4,320,512]{2,1,0:T(8,128)(2,1)} %param.35), channel_id=1, source_target_pairs={{0,240},{4,244},{8,248},{12,252},{16,224},{20,228},{24,232},{28,23... | collective-permute-start | bytes 3932168 | tf_op jit(solution)/shard_map/while/body/cond/branch_15_fun/ppermute | solution.py:19
  86.4 31.5 %collective-permute-done.29 = bf16[4,320,512]{2,1,0:T(8,128)(2,1)} collective-permute-done((bf16[4,320,512]{2,1,0:T(8,128)(2,1)}, bf16[4,320,512]{2,1,0:T(8,128)(2,1)}, u32[]{:S(2)}, u32[]{:S(2)}) %collective-permute-start.29) | collective-permute-done | bytes 1310752 | tf_op jit(solution)/shard_map/while/body/cond/branch_15_fun/ppermute | solution.py:19
  117.9 2.5 %conditional.11 = (bf16[4,640,512]{2,1,0:T(8,128)(2,1)}) conditional(s32[]{:T(128)} %convert_element_type.9, (s32[]{:T(128)}, bf16[4,640,512]{2,1,0:T(8,128)(2,1)}, bf16[4,320,512]{2,1,0:T(8,128)(2,1)}) %tuple.168, (bf16[4,320,512]{2,1,0:T(8,128)(2,1)}, s32[]{:T(128)}, bf16[4,640,512]{2,1,0:T(8,128)(2,1)}) %tuple.169), branch_computations={%region_37.37_spmd, %region_38.38_spmd} | conditional | flops 4 | bytes 7864418 | solution.py:142
  117.9 2.5 %constant_dynamic-update-slice_fusion.2 = bf16[4,640,512]{2,1,0:T(8,128)(2,1)} fusion(bf16[4,640,512]{2,1,0:T(8,128)(2,1)} %get-tuple-element.154, bf16[4,320,512]{2,1,0:T(8,128)(2,1)} %get-tuple-element.155, s32[]{:T(128)S(6)} %select_n.27), kind=kLoop, calls=%fused_computation.2 | loop fusion | bytes 2621444 | tf_op jit(solution)/shard_map/while/body/cond/branch_0_fun/dynamic_update_slice | solution.py:136
  120.4 5.3 %shard_map.51 = (f32[640,1]{1,0:T(8,128)S(1)}, bf16[640,640]{1,0:T(8,128)(2,1)S(1)}, bf16[320,512]{1,0:T(8,128)(2,1)S(1)}, bf16[320,512]{1,0:T(8,128)(2,1)S(1)}) custom-call(bf16[640,512]{1,0:T(8,128)(2,1)S(1)} %copy-done, bf16[640,512]{1,0:T(8,128)(2,1)S(1)} %collective-permute-done.37.refs_1_, bf16[640,512]{1,0:T(8,128)(2,1)S(1)} %collective-permute-done.38.refs_2_, ...), custom_call_target="tpu_custom_call" | custom-call | tf_op jit(solution)/shard_map/pallas_call | solution.py:173
  130.0 6.5 %collective-permute-done.40.refs_2_ = bf16[320,512]{1,0:T(8,128)(2,1)S(1)} collective-permute-done((bf16[320,512]{1,0:T(8,128)(2,1)S(1)}, bf16[320,512]{1,0:T(8,128)(2,1)S(1)}, u32[]{:S(2)}, u32[]{:S(2)}) %collective-permute-start.40) | collective-permute-done | bytes 327712 | tf_op jit(solution)/shard_map/ppermute | solution.py:14
  138.7 4.8 %collective-permute-done.42.refs_2_ = bf16[320,512]{1,0:T(8,128)(2,1)S(1)} collective-permute-done((bf16[320,512]{1,0:T(8,128)(2,1)S(1)}, bf16[320,512]{1,0:T(8,128)(2,1)S(1)}, u32[]{:S(2)}, u32[]{:S(2)}) %collective-permute-start.42) | collective-permute-done | bytes 327712 | tf_op jit(solution)/shard_map/ppermute | solution.py:14
  147.8 25.6 %all_to_all.6 = f32[4,1,640]{2,1,0:T(1,128)S(1)} all-to-all(f32[4,1,640]{2,1,0:T(1,128)S(1)} %broadcast_in_dim.8), channel_id=1, replica_groups=mesh['blk'=64,'grp'=4] {'grp'}, dimensions={0} | all-to-all | bytes 20480 | tf_op jit(solution)/shard_map/all_to_all | solution.py:216
  (42 shorter events, 23.3 us)
Async XLA Ops:
  2.2 5.6 %copy-start.2 = (s32[2,64]{1,0:T(2,128)S(1)}, s32[2,64]{1,0:T(2,128)}, u32[]{:S(2)}) copy-start(s32[2,64]{1,0:T(2,128)} %param.45) | copy-start | bytes 1540
  2.2 16.0 %collective-permute-start.32 = (bf16[320,512]{1,0:T(8,128)(2,1)S(1)}, bf16[320,512]{1,0:T(8,128)(2,1)S(1)}, u32[]{:S(2)}, u32[]{:S(2)}) collective-permute-start(bf16[320,512]{1,0:T(8,128)(2,1)S(1)} %pad_maximum_fusion.4), channel_id=1, source_target_pairs={{0,1},{1,0},{2,3},{3,2},{4,5},{5,4},{6,7},{7,6},{8,9},{9,8},{10,11... | collective-permute-start | bytes 983048 | tf_op jit(solution)/shard_map/ppermute | solution.py:14
  4.3 23.0 %collective-permute-start.33 = (bf16[320,512]{1,0:T(8,128)(2,1)S(1)}, bf16[320,512]{1,0:T(8,128)(2,1)S(1)}, u32[]{:S(2)}, u32[]{:S(2)}) collective-permute-start(bf16[320,512]{1,0:T(8,128)(2,1)S(1)} %pad_maximum_fusion.5), channel_id=1, source_target_pairs={{0,2},{1,3},{2,0},{3,1},{4,6},{5,7},{6,4},{7,5},{8,10},{9,11},{10,... | collective-permute-start | bytes 983048 | tf_op jit(solution)/shard_map/ppermute | solution.py:14
  7.6 23.0 %collective-permute-start.34 = (bf16[320,512]{1,0:T(8,128)(2,1)S(1)}, bf16[320,512]{1,0:T(8,128)(2,1)S(1)}, u32[]{:S(2)}, u32[]{:S(2)}) collective-permute-start(bf16[320,512]{1,0:T(8,128)(2,1)S(1)} %pad_maximum_fusion.6), channel_id=1, source_target_pairs={{0,3},{1,2},{2,1},{3,0},{4,7},{5,6},{6,5},{7,4},{8,11},{9,10},{10,... | collective-permute-start | bytes 983048 | tf_op jit(solution)/shard_map/ppermute | solution.py:14
  19.1 61.8 %collective-permute-start.36 = (bf16[2,320,512]{2,1,0:T(8,128)(2,1)}, bf16[2,320,512]{2,1,0:T(8,128)(2,1)}, u32[]{:S(2)}, u32[]{:S(2)}) collective-permute-start(bf16[2,320,512]{2,1,0:T(8,128)(2,1)} %pad_maximum_fusion.3), channel_id=1, source_target_pairs={{0,11},{1,10},{2,9},{3,8},{4,15},{5,14},{6,13},{7,12},{8,3},{9,2},... | collective-permute-start | bytes 1966088 | tf_op jit(solution)/shard_map/ppermute | solution.py:29
  31.5 49.4 %collective-permute-start.35 = (bf16[2,320,512]{2,1,0:T(8,128)(2,1)}, bf16[2,320,512]{2,1,0:T(8,128)(2,1)}, u32[]{:S(2)}, u32[]{:S(2)}) collective-permute-start(bf16[2,320,512]{2,1,0:T(8,128)(2,1)} %pad_maximum_fusion.2), channel_id=1, source_target_pairs={{0,11},{1,10},{2,9},{3,8},{4,15},{5,14},{6,13},{7,12},{8,3},{9,2},... | collective-permute-start | bytes 1966088 | tf_op jit(solution)/shard_map/ppermute | solution.py:29
  35.8 1.1 copy-start
  36.9 83.5 %collective-permute-start.38 = (bf16[640,512]{1,0:T(8,128)(2,1)S(1)}, bf16[640,512]{1,0:T(8,128)(2,1)S(1)}, u32[]{:S(2)}, u32[]{:S(2)}) collective-permute-start(bf16[640,512]{1,0:T(8,128)(2,1)S(1)} %copy-done), channel_id=1, source_target_pairs={{0,2},{1,3},{2,0},{3,1},{4,6},{5,7},{6,4},{7,5},{8,10},{9,11},{10,... | collective-permute-start | bytes 1966088 | tf_op jit(solution)/shard_map/ppermute | solution.py:14
  44.4 76.0 %collective-permute-start.39 = (bf16[640,512]{1,0:T(8,128)(2,1)S(1)}, bf16[640,512]{1,0:T(8,128)(2,1)S(1)}, u32[]{:S(2)}, u32[]{:S(2)}) collective-permute-start(bf16[640,512]{1,0:T(8,128)(2,1)S(1)} %copy-done), channel_id=1, source_target_pairs={{0,3},{1,2},{2,1},{3,0},{4,7},{5,6},{6,5},{7,4},{8,11},{9,10},{10,... | collective-permute-start | bytes 1966088 | tf_op jit(solution)/shard_map/ppermute | solution.py:14
  46.3 28.7 %collective-permute-start = (bf16[4,320,512]{2,1,0:T(8,128)(2,1)S(1)}, bf16[4,320,512]{2,1,0:T(8,128)(2,1)}, u32[]{:S(2)}, u32[]{:S(2)}) collective-permute-start(bf16[4,320,512]{2,1,0:T(8,128)(2,1)S(1)} %param.1), channel_id=1, source_target_pairs={{0,16},{4,20},{8,24},{12,28},{16,0},{20,4},{24,8},{28,12},{32,48},... | collective-permute-start | bytes 3932168 | tf_op jit(solution)/shard_map/while/body/cond/branch_1_fun/ppermute | solution.py:19
  75.1 3.4 %collective-permute-start.30 = (bf16[4,320,512]{2,1,0:T(8,128)(2,1)}, bf16[4,320,512]{2,1,0:T(8,128)(2,1)}, u32[]{:S(2)}, u32[]{:S(2)}) collective-permute-start(bf16[4,320,512]{2,1,0:T(8,128)(2,1)} %get-tuple-element.144), channel_id=1, source_target_pairs={{0,4},{4,0},{8,12},{12,8},{16,20},{20,16},{24,28},{28,24},{32,36},... | collective-permute-start | bytes 3932168 | tf_op jit(solution)/shard_map/while/body/cond/branch_1_fun/ppermute | solution.py:19
  80.9 39.5 %collective-permute-start.37 = (bf16[640,512]{1,0:T(8,128)(2,1)S(1)}, bf16[640,512]{1,0:T(8,128)(2,1)S(1)}, u32[]{:S(2)}, u32[]{:S(2)}) collective-permute-start(bf16[640,512]{1,0:T(8,128)(2,1)S(1)} %copy-done), channel_id=1, source_target_pairs={{0,1},{1,0},{2,3},{3,2},{4,5},{5,4},{6,7},{7,6},{8,9},{9,8},{10,11... | collective-permute-start | bytes 1966088 | tf_op jit(solution)/shard_map/ppermute | solution.py:14
  83.5 34.5 %collective-permute-start.29 = (bf16[4,320,512]{2,1,0:T(8,128)(2,1)}, bf16[4,320,512]{2,1,0:T(8,128)(2,1)}, u32[]{:S(2)}, u32[]{:S(2)}) collective-permute-start(bf16[4,320,512]{2,1,0:T(8,128)(2,1)} %param.35), channel_id=1, source_target_pairs={{0,240},{4,244},{8,248},{12,252},{16,224},{20,228},{24,232},{28,23... | collective-permute-start | bytes 3932168 | tf_op jit(solution)/shard_map/while/body/cond/branch_15_fun/ppermute | solution.py:19
  120.4 7.5 %copy-start.1 = (bf16[4,640,512]{2,1,0:T(8,128)(2,1)S(1)}, bf16[4,640,512]{2,1,0:T(8,128)(2,1)}, u32[]{:S(2)}) copy-start(bf16[4,640,512]{2,1,0:T(8,128)(2,1)} %get-tuple-element.207.refs_4_.refs_1_) | copy-start | bytes 7864324
  125.8 10.7 %collective-permute-start.40 = (bf16[320,512]{1,0:T(8,128)(2,1)S(1)}, bf16[320,512]{1,0:T(8,128)(2,1)S(1)}, u32[]{:S(2)}, u32[]{:S(2)}) collective-permute-start(bf16[320,512]{1,0:T(8,128)(2,1)S(1)} %get-tuple-element.211), channel_id=1, source_target_pairs={{0,1},{1,0},{2,3},{3,2},{4,5},{5,4},{6,7},{7,6},{8,9},{9,8},{10,11... | collective-permute-start | bytes 983048 | tf_op jit(solution)/shard_map/ppermute | solution.py:14
  127.6 15.9 %collective-permute-start.42 = (bf16[320,512]{1,0:T(8,128)(2,1)S(1)}, bf16[320,512]{1,0:T(8,128)(2,1)S(1)}, u32[]{:S(2)}, u32[]{:S(2)}) collective-permute-start(bf16[320,512]{1,0:T(8,128)(2,1)S(1)} %get-tuple-element.215), channel_id=1, source_target_pairs={{0,1},{1,0},{2,3},{3,2},{4,5},{5,4},{6,7},{7,6},{8,9},{9,8},{10,11... | collective-permute-start | bytes 983048 | tf_op jit(solution)/shard_map/ppermute | solution.py:14
  136.9 37.1 %collective-permute-start.41 = (bf16[640,512]{1,0:T(8,128)(2,1)}, bf16[640,512]{1,0:T(8,128)(2,1)S(1)}, u32[]{:S(2)}, u32[]{:S(2)}) collective-permute-start(bf16[640,512]{1,0:T(8,128)(2,1)} %get-tuple-element.214), channel_id=1, source_target_pairs={{0,1},{1,0},{2,3},{3,2},{4,5},{5,4},{6,7},{7,6},{8,9},{9,8},{10,11... | collective-permute-start | bytes 1966088 | tf_op jit(solution)/shard_map/ppermute | solution.py:14
  144.7 29.3 %collective-permute-start.43 = (bf16[320,512]{1,0:T(8,128)(2,1)}, bf16[320,512]{1,0:T(8,128)(2,1)S(1)}, u32[]{:S(2)}, u32[]{:S(2)}) collective-permute-start(bf16[320,512]{1,0:T(8,128)(2,1)} %shard_map.54), channel_id=1, source_target_pairs={{0,2},{1,3},{2,0},{3,1},{4,6},{5,7},{6,4},{7,5},{8,10},{9,11},{10,... | collective-permute-start | bytes 983048 | tf_op jit(solution)/shard_map/ppermute | solution.py:14
  146.9 27.2 %collective-permute-start.44 = (bf16[320,512]{1,0:T(8,128)(2,1)S(1)}, bf16[320,512]{1,0:T(8,128)(2,1)S(1)}, u32[]{:S(2)}, u32[]{:S(2)}) collective-permute-start(bf16[320,512]{1,0:T(8,128)(2,1)S(1)} %shard_map.53), channel_id=1, source_target_pairs={{0,2},{1,3},{2,0},{3,1},{4,6},{5,7},{6,4},{7,5},{8,10},{9,11},{10,... | collective-permute-start | bytes 983048 | tf_op jit(solution)/shard_map/ppermute | solution.py:14
